TPU v7x, 32 devices: a whole 2x2x4 slice. The times are simulated.
32 devices in a mesh: dir: 2 (over x), row: 16 (over z, y, core).
Axes of the slice: x: 2, y: 2, z: 4, core: 2. Of those that a mesh axis runs over, the one named last changes fastest.
Arguments:
- white_noise: bfloat16 [2, 8192, 8192], P(None, ('dir', 'row')), may hold values from -6 to 6
- geometry: int32 [2, 2], P('dir'), may hold values from 0 to 3
- window: int32 [2], P('dir'), may hold values from 1 to 8, as said below
- tile_map: int32 [2, 512], P('dir'), may hold values from 0 to 16383
- link_gain: float32 [2, 512], P('dir'), may hold values from 0.1 to 1
- serving: int32 [512], replicated, may hold values from 0 to 1
Outputs:
- fluctuation: float32 [2, 128, 128], P('dir', 'row')
- signal_ratio: float32 [512], P(('dir', 'row'))
Inputs may be any that keep to these rules, and one draw needn't show every extreme that they name: geometry[d,0] is direction d's Fresnel-scale bin and geometry[d,1] its slant bin. `window`: some direction has the half-width 8. `tile_map`: tile (t,u) is numbered t * 128 + u.
All inputs are finite; a program needn't handle non-finite values.
Results may differ from a plain program's by a relative error of at most 0.034.
Values may be sent and summed in bfloat16 or wider, within the bound.
A program may use at most 64 MiB of HBM per device.

v0:
```python
import math

import jax
import jax.numpy as jnp
import ml_dtypes
import numpy as np
from jax import lax
from jax.experimental import pallas as pl
from jax.experimental.pallas import tpu as pltpu
from jax.sharding import PartitionSpec as P

N = 8192
FIRST = 64
SECOND = 128
ROWS_DEV = 32
XTILES = 128
YTILES = 8
TILE_X = 64
GROUP = 8
CHUNKS = 4


full_turn = 2.0 * math.pi
noise_floor = 0.05
tiny_value = 1e-06
strength = 1.6
row_patterns = (
    "zrab,zwak->wrkb",
    "zrkb,zwbc->wrkc",
    "zrkc,wzbc->wrkb",
    "zrkb,wzak->wrab",
    "zrkb,zak->rab",
)
column_patterns = (
    "zaby,zwak->wkby",
    "zkby,zwbc->wkcy",
    "zkcy,wzbc->wkby",
    "zkby,wzak->waby",
    "zkby,zak->aby",
)


def complex_block(real_part, imag_part):
    return jnp.stack(
        [jnp.stack([real_part, imag_part]), jnp.stack([-imag_part, real_part])]
    ).astype(jnp.bfloat16)


def transform_tables(first, second):
    total = first * second
    outer_ids = jnp.arange(first, dtype=jnp.int32)
    inner_ids = jnp.arange(second, dtype=jnp.int32)
    outer_angle = (outer_ids[:, None] * outer_ids[None, :] % first).astype(jnp.float32) * (
        full_turn / first
    )
    inner_angle = (inner_ids[:, None] * inner_ids[None, :] % second).astype(jnp.float32) * (
        full_turn / second
    )
    twist_angle = (outer_ids[:, None] * inner_ids[None, :] % total).astype(jnp.float32) * (
        full_turn / total
    )
    return (
        complex_block(jnp.cos(outer_angle), -jnp.sin(outer_angle)),
        complex_block(jnp.cos(inner_angle), -jnp.sin(inner_angle)),
        jnp.cos(twist_angle),
        -jnp.sin(twist_angle),
    )


def signed_wave(positions, first, second):
    total = first * second
    wave_number = positions // second + first * (positions % second)
    return jnp.where(wave_number >= total // 2, wave_number - total, wave_number).astype(
        jnp.float32
    )


def spectral_filter(row_ids, column_ids):
    wave_rows = signed_wave(row_ids, FIRST, SECOND)
    wave_columns = signed_wave(column_ids, FIRST, SECOND)
    squared_radius = 16.0 + wave_rows[:, None] ** 2 + wave_columns[None, :] ** 2
    return strength * float(N) * float(N) * squared_radius ** (-0.75)


def fresnel_factor(geometry_row, first, second):
    total = first * second
    fresnel_area = 144.0 * jnp.exp2(geometry_row[0].astype(jnp.float32))
    positions = jnp.arange(total, dtype=jnp.int32).reshape(first, second)
    scaled = signed_wave(positions, first, second) * (full_turn / total)
    turning = 0.5 * scaled * scaled * fresnel_area
    return (jnp.cos(turning), -jnp.sin(turning))


def complex_times(values, real_part, imag_part):
    return jnp.stack(
        [
            values[0] * real_part - values[1] * imag_part,
            values[0] * imag_part + values[1] * real_part,
        ]
    )


def contract(pattern, operand, matrix):
    return jnp.einsum(pattern, operand, matrix, preferred_element_type=jnp.float32)


def table_length(tables):
    return tables[0].shape[2] * tables[1].shape[2]


def forward_axis(values, tables, factor, patterns, trailing):
    outer_table, inner_table, twist_real, twist_imag = tables
    factor_real, factor_imag = factor
    if trailing:
        twist_real, twist_imag = (twist_real[..., None], twist_imag[..., None])
        factor_real, factor_imag = (factor_real[..., None], factor_imag[..., None])
    section_one = complex_times(
        contract(patterns[0], values, outer_table), twist_real, twist_imag
    ).astype(jnp.bfloat16)
    section_two = contract(patterns[1], section_one, inner_table)
    return complex_times(section_two, factor_real, factor_imag).astype(jnp.bfloat16)


def inverse_first(values, tables, patterns, trailing):
    outer_table, inner_table, twist_real, twist_imag = tables
    if trailing:
        twist_real, twist_imag = (twist_real[..., None], twist_imag[..., None])
    return complex_times(
        contract(patterns[2], values, inner_table), twist_real, -twist_imag
    ).astype(jnp.bfloat16)


def inverse_axis(values, tables, patterns, trailing):
    section_one = inverse_first(values, tables, patterns, trailing)
    return contract(patterns[3], section_one, tables[0]) * (1.0 / table_length(tables))


def window_matrix(half_width):
    positions = jnp.arange(XTILES, dtype=jnp.int32)
    difference = (positions[:, None] - positions[None, :]) % XTILES
    distance = jnp.minimum(difference, XTILES - difference)
    return (distance <= half_width).astype(jnp.float32)


def tile_statistics(first_moment, second_moment, half_width, tile_rows):
    window_mask = window_matrix(half_width)
    cells = ((2 * half_width + 1) * (TILE_X * tile_rows)).astype(jnp.float32)
    mean_one = jnp.dot(first_moment, window_mask, precision=lax.Precision.HIGHEST) / cells
    mean_two = jnp.dot(second_moment, window_mask, precision=lax.Precision.HIGHEST) / cells
    fluctuation = mean_two / (mean_one * mean_one + tiny_value) - 1.0
    return (fluctuation, mean_one * jnp.exp(-fluctuation))


def propagate_columns(phase_patch, tables_y, slant_factor, fresnel_y):
    patch_rows = phase_patch.shape[0]
    width_here = phase_patch.shape[1]
    outer_len = tables_y[0].shape[2]
    inner_len = tables_y[1].shape[2]
    turned_phase = slant_factor * phase_patch
    screen_field = jnp.stack([jnp.cos(turned_phase), jnp.sin(turned_phase)]).astype(jnp.bfloat16)
    stacked = screen_field.reshape(2, outer_len, inner_len, width_here)
    spectral = forward_axis(stacked, tables_y, fresnel_y, column_patterns, True)
    result = inverse_axis(spectral, tables_y, column_patterns, True)
    return result.astype(jnp.bfloat16).reshape(2, patch_rows, width_here)


def half_screen_rows(white_noise, row_start, tables):
    rows_here = white_noise.shape[1]
    row_ids = row_start + jnp.arange(rows_here, dtype=jnp.int32)
    column_ids = jnp.arange(N, dtype=jnp.int32)
    spectral_gain = spectral_filter(row_ids, column_ids)
    spectrum = (white_noise.astype(jnp.float32) * spectral_gain).astype(jnp.bfloat16)
    half_screen = inverse_axis(
        spectrum.reshape(2, rows_here, FIRST, SECOND), tables, row_patterns, False
    )
    half_screen = half_screen.astype(jnp.bfloat16).reshape(2, rows_here, N)
    return half_screen


def gathered_patch(half_screen, geometry, tables, patch_len):
    turned = lax.all_to_all(half_screen, "row", split_axis=2, concat_axis=1, tiled=True)
    band_rows = turned.shape[1]
    columns = turned.shape[2]
    offset_rows = N // 4 * geometry[0, 1]
    blocks = band_rows // SECOND
    block_start = lax.axis_index("dir") * blocks
    stacked = turned.reshape(2, blocks, SECOND, columns)
    twist_real = lax.dynamic_slice_in_dim(tables[2], block_start, blocks, 0)[..., None]
    twist_imag = lax.dynamic_slice_in_dim(tables[3], block_start, blocks, 0)[..., None]
    section_one = complex_times(
        contract("zkcx,wzbc->wkbx", stacked, tables[1]), twist_real, -twist_imag
    )
    section_one = section_one.astype(jnp.bfloat16)
    outer_count = patch_len // SECOND
    outer_ids = (offset_rows // SECOND + jnp.arange(outer_count, dtype=jnp.int32)) % FIRST
    patch_outer = jnp.take(tables[0][0], outer_ids, axis=1)
    phase_patch = contract(
        "zkbx,zak->abx", lax.all_gather(section_one, "dir", axis=1, tiled=True), patch_outer
    )
    return phase_patch.reshape(patch_len, columns) * (1.0 / N)


def host_tables():
    def block(length):
        ids = np.arange(length)
        angle = (ids[:, None] * ids[None, :] % length) * (full_turn / length)
        real_part, imag_part = (np.cos(angle), np.sin(angle))
        return np.array([[real_part, -imag_part], [imag_part, real_part]])

    inner = block(SECOND).transpose(1, 3, 0, 2).reshape(2 * SECOND, 2 * SECOND)
    outer = block(FIRST).transpose(0, 2, 1, 3).reshape(2 * FIRST, 2 * FIRST)
    spread = np.kron(outer, np.eye(GROUP))
    twist = np.arange(FIRST)[:, None] * np.arange(SECOND)[None, :] * (full_turn / N)
    twist = np.repeat(twist, GROUP, axis=0)
    angle = (np.arange(SECOND)[:, None] * np.arange(SECOND)[None, :] % SECOND) * (full_turn / SECOND)
    return (
        inner.astype(ml_dtypes.bfloat16),
        np.stack([np.cos(twist), np.sin(twist)]).astype(np.float32),
        spread.astype(ml_dtypes.bfloat16),
        np.stack([np.cos(angle), np.sin(angle)]).astype(np.float32),
    )


def screen_kernel(
    spot, noise, rows_squared, columns_squared, inner, twist, spread, kept, moved, staged
):
    core, y_spot = (spot[0], spot[1])
    root = lax.rsqrt(16.0 + rows_squared[...] + columns_squared[...])
    gain = strength * root * (root * lax.rsqrt(root))
    spectrum = [noise[z].astype(jnp.float32) * gain for z in range(2)]
    sections = []
    for group in range(2):
        rows = slice(group * GROUP, (group + 1) * GROUP)
        parts = [
            jnp.concatenate(
                [spectrum[z][rows, k * SECOND : (k + 1) * SECOND] for k in range(FIRST)], axis=0
            ).astype(jnp.bfloat16)
            for z in range(2)
        ]
        first = jnp.dot(
            jnp.concatenate(parts, axis=1), inner[...], preferred_element_type=jnp.float32
        )
        real_part, imag_part = (first[:, :SECOND], first[:, SECOND:])
        turned = jnp.concatenate(
            [
                real_part * twist[0] - imag_part * twist[1],
                real_part * twist[1] + imag_part * twist[0],
            ],
            axis=0,
        )
        sections.append(turned.astype(jnp.bfloat16))
    staged[...] = jnp.dot(
        spread[...], jnp.concatenate(sections, axis=1), preferred_element_type=jnp.float32
    )
    for core_side, target in enumerate((kept, moved)):
        for y_side in range(2):
            for chunk in range(CHUNKS):
                for z_spot in range(4):
                    place = z_spot * 4 + (y_spot ^ y_side) * 2 + (core ^ core_side)
                    for w in range(2):
                        start = (w * FIRST + place * CHUNKS + chunk) * GROUP
                        taken = staged[pl.ds(pl.multiple_of(start, GROUP), GROUP), :]
                        both = jnp.concatenate([taken[:, :SECOND], taken[:, SECOND:]], axis=0)
                        target[y_side, chunk, w, :, z_spot * SECOND : (z_spot + 1) * SECOND] = (
                            both.astype(jnp.bfloat16)
                        )


def half_screens(white_noise, row_start, row, host):
    rows_here = white_noise.shape[1]
    inner, twist, spread, _ = host
    row_waves = signed_wave(row_start + jnp.arange(rows_here, dtype=jnp.int32), FIRST, SECOND)
    column_waves = signed_wave(jnp.arange(N, dtype=jnp.int32), FIRST, SECOND)
    spot = jnp.stack([row % 2, row // 2 % 2])
    step = 2 * GROUP
    out_shape = (2, CHUNKS, 2, rows_here, 4 * SECOND)
    out_spec = pl.BlockSpec((2, CHUNKS, 2, step, 4 * SECOND), lambda i: (0, 0, 0, i, 0))

    def whole(array):
        return pl.BlockSpec(array.shape, lambda i: (0,) * array.ndim)

    return pl.pallas_call(
        screen_kernel,
        grid=(rows_here // step,),
        in_specs=[
            pl.BlockSpec(memory_space=pltpu.SMEM),
            pl.BlockSpec((2, step, N), lambda i: (0, i, 0)),
            pl.BlockSpec((step, 1), lambda i: (i, 0)),
            pl.BlockSpec((1, N), lambda i: (0, 0)),
            whole(inner),
            whole(twist),
            whole(spread),
        ],
        out_specs=[out_spec, out_spec],
        out_shape=[jax.ShapeDtypeStruct(out_shape, jnp.bfloat16)] * 2,
        scratch_shapes=[pltpu.VMEM((2 * FIRST * GROUP, 2 * SECOND), jnp.float32)],
        compiler_params=pltpu.CompilerParams(vmem_limit_bytes=48 * 1024 * 1024),
        cost_estimate=pl.CostEstimate(
            flops=20_000_000_000, bytes_accessed=20_000_000, transcendentals=4_000_000
        ),
    )(
        spot,
        white_noise,
        (row_waves * row_waves)[:, None],
        (column_waves * column_waves)[None, :],
        inner,
        twist,
        spread,
    )


def matrix_kernel(slow, fast, matrix):
    for source in range(2):
        for near in range(2):
            block = source * 2 + near
            slow_real = slow[0, :, block : block + 1]
            slow_imag = slow[1, :, block : block + 1]
            real_part = slow_real * fast[0] - slow_imag * fast[1]
            imag_part = slow_real * fast[1] + slow_imag * fast[0]
            for z, part in enumerate((real_part, -imag_part)):
                start = ((source * 2 + z) * 2 + near) * SECOND
                matrix[:, start : start + SECOND] = part.astype(jnp.bfloat16)


def patch_matrix(slant_bins, block_ids, outer_count, fast):
    inner_ids = jnp.arange(SECOND, dtype=jnp.int32)
    outer_ids = slant_bins[:, None] * (FIRST // 4) + jnp.arange(outer_count, dtype=jnp.int32)
    position = (outer_ids[:, :, None] * SECOND + inner_ids).reshape(-1)
    slow = (position[:, None] * block_ids[None, :] % N).astype(jnp.float32) * (full_turn / N)
    slow = jnp.stack([jnp.cos(slow), jnp.sin(slow)])
    length = position.shape[0]
    return pl.pallas_call(
        matrix_kernel,
        grid=(length // SECOND,),
        in_specs=[
            pl.BlockSpec((2, SECOND, 4), lambda i: (0, i, 0)),
            pl.BlockSpec(fast.shape, lambda i: (0, 0, 0)),
        ],
        out_specs=pl.BlockSpec((SECOND, 8 * SECOND), lambda i: (i, 0)),
        out_shape=jax.ShapeDtypeStruct((length, 8 * SECOND), jnp.bfloat16),
        cost_estimate=pl.CostEstimate(
            flops=8_000_000, bytes_accessed=4_000_000, transcendentals=0
        ),
    )(slow, fast)


def product_kernel(matrix, kept, received, *rest):
    *added, result = rest
    depth = kept.shape[0] * kept.shape[1]
    total = jnp.dot(
        matrix[:, :depth],
        kept[...].reshape(depth, kept.shape[2]),
        preferred_element_type=jnp.float32,
    )
    total += jnp.dot(
        matrix[:, depth:],
        received[...].reshape(depth, kept.shape[2]),
        preferred_element_type=jnp.float32,
    )
    for term in added:
        total += term[...].astype(jnp.float32)
    result[...] = total.astype(result.dtype)


def patch_product(matrix, bins, kept, received, sides, chunk, *added):
    patch_len = matrix.shape[0] // 2
    _, _, parts, rows, columns = kept.shape
    bin_start, bin_count = bins
    side_start, side_count = sides
    values_spec = pl.BlockSpec(
        (None, None, parts, rows, columns), lambda i, j: (side_start + j, chunk, 0, 0, 0)
    )
    result_spec = pl.BlockSpec(
        (None, patch_len, columns), lambda i, j: (i * side_count + j, 0, 0)
    )
    count = bin_count * side_count
    return pl.pallas_call(
        product_kernel,
        grid=(bin_count, side_count),
        in_specs=[
            pl.BlockSpec((patch_len, matrix.shape[1]), lambda i, j: (bin_start + i, 0)),
            values_spec,
            values_spec,
        ]
        + [result_spec] * len(added),
        out_specs=result_spec,
        out_shape=jax.ShapeDtypeStruct((count, patch_len, columns), jnp.bfloat16),
        compiler_params=pltpu.CompilerParams(vmem_limit_bytes=32 * 1024 * 1024),
        cost_estimate=pl.CostEstimate(
            flops=2 * count * patch_len * matrix.shape[1] * columns,
            bytes_accessed=4_000_000,
            transcendentals=0,
        ),
    )(matrix, kept, received, *added)


def reduced_patch(white_noise, row_start, geometry):
    row_count = lax.axis_size("row")
    patch_len = row_count * ROWS_DEV
    row = lax.axis_index("row")
    z_spot = row // 4
    over_core = [(r, r ^ 1) for r in range(row_count)]
    over_y = [(r, r ^ 2) for r in range(row_count)]
    over_x = [(0, 1), (1, 0)]
    host = host_tables()
    other_bin = lax.ppermute(geometry[0, 1], "dir", over_x)
    kept, moved = half_screens(white_noise, row_start, row, host)
    received = lax.ppermute(moved, "row", over_core)
    first_block = 2 * (lax.axis_index("dir") * row_count + row)
    other_block = 2 * (lax.axis_index("dir") * row_count + (row ^ 1))
    block_ids = jnp.stack([first_block, first_block + 1, other_block, other_block + 1])
    slant_bins = jnp.stack([geometry[0, 1], other_bin])
    matrix = patch_matrix(slant_bins, block_ids, patch_len // SECOND, host[3])
    own, other, both = ((0, 1), (1, 1), (0, 2))

    def product(bins, sides, chunk, *added):
        return patch_product(matrix, bins, kept, received, sides, chunk, *added)

    def over(first_x, values):
        if first_x:
            return lax.ppermute(values, "dir", over_x)
        return lax.ppermute(values, "row", over_y)

    arrived = {}
    for chunk in range(CHUNKS):
        first_x = chunk % 2 == 0
        leaving = product(other, both, chunk) if first_x else product(both, other, chunk)
        if chunk >= 2:
            leaving, _ = lax.optimization_barrier((leaving, arrived[chunk - 2]))
        arrived[chunk] = over(first_x, leaving)
    totals = []
    for chunk in range(CHUNKS):
        first_x = chunk % 2 == 0
        first_kept, first_moved = (arrived[chunk][:1], arrived[chunk][1:])
        if first_x:
            second = product(own, other, chunk, first_moved)
        else:
            second = product(other, own, chunk, first_moved)
        second = over(not first_x, second)
        total = product(own, own, chunk, first_kept, second)[0]

        def slice_for(spot):
            return lax.dynamic_slice_in_dim(total, spot * SECOND, SECOND, 1)

        result = slice_for(z_spot).astype(jnp.float32)
        for shift in range(1, 4):
            pairs = [(r, r ^ (4 * shift)) for r in range(row_count)]
            sent = lax.ppermute(slice_for(z_spot ^ shift), "row", pairs)
            result = result + sent.astype(jnp.float32)
        totals.append(result)
    return jnp.concatenate(totals, axis=1)


def body(white_noise, geometry, window, tile_map, link_gain, serving):
    row_count = lax.axis_size("row")
    tables = transform_tables(FIRST, SECOND)
    tables_y = transform_tables(row_count, ROWS_DEV)
    patch_len = row_count * ROWS_DEV
    rows_here = white_noise.shape[1]
    row_start = lax.axis_index(("dir", "row")) * rows_here
    slant_factor = 1.0 + 0.25 * geometry[0, 1].astype(jnp.float32)
    fresnel_x = fresnel_factor(geometry[0], FIRST, SECOND)
    fresnel_y = fresnel_factor(geometry[0], row_count, ROWS_DEV)
    if lax.axis_size("dir") == 2 and row_count == 16 and rows_here == 2 * SECOND:
        phase_patch = reduced_patch(white_noise, row_start, geometry)
    else:
        half_screen = half_screen_rows(white_noise, row_start, tables)
        phase_patch = gathered_patch(half_screen, geometry, tables, patch_len)
    columns = phase_patch.shape[1]
    screen_field = propagate_columns(phase_patch, tables_y, slant_factor, fresnel_y)
    stacked_field = screen_field.reshape(2, row_count, ROWS_DEV, columns)
    portion = lax.all_to_all(stacked_field, "row", split_axis=1, concat_axis=3, tiled=True)
    item_count = portion.shape[2]
    stacked = portion.reshape(2, item_count, FIRST, SECOND)
    spectral = forward_axis(stacked, tables, fresnel_x, row_patterns, False)
    wave_field = inverse_axis(spectral, tables, row_patterns, False)
    intensity = wave_field[0] * wave_field[0] + wave_field[1] * wave_field[1]
    intensity = intensity.reshape(item_count, XTILES, TILE_X)
    tile_one = jnp.sum(intensity, axis=2)
    tile_two = jnp.sum(intensity * intensity, axis=2)
    tile_rows = ROWS_DEV // YTILES
    first_moment = jnp.sum(tile_one.reshape(YTILES, tile_rows, XTILES), axis=1)
    second_moment = jnp.sum(tile_two.reshape(YTILES, tile_rows, XTILES), axis=1)
    fluctuation, faded_power = tile_statistics(first_moment, second_moment, window[0], tile_rows)
    faded_flat = faded_power.reshape(-1)
    tile_total = faded_flat.shape[0]
    local_tile = tile_map[0] - lax.axis_index("row") * tile_total
    inside = (local_tile >= 0) & (local_tile < tile_total)
    looked = jnp.where(inside, jnp.take(faded_flat, jnp.clip(local_tile, 0, tile_total - 1)), 0.0)
    received = link_gain[0] * looked
    direction = lax.axis_index("dir")
    serves_here = serving == direction
    signal_part = jnp.where(serves_here, received, 0.0)
    interference_part = jnp.where(serves_here, 0.0, received)
    device_count = lax.axis_size(("dir", "row"))
    terms = jnp.stack([signal_part, interference_part]).reshape(2, device_count, -1)
    gathered = lax.all_to_all(
        terms.transpose(1, 0, 2), ("dir", "row"), split_axis=0, concat_axis=0, tiled=True
    )
    signal, interference = jnp.sum(gathered, axis=0)
    signal_ratio = jnp.log10(signal / (interference + noise_floor))
    return (fluctuation[None], signal_ratio)


def solution(mesh):
    return jax.shard_map(
        body,
        mesh=mesh,
        in_specs=(
            P(None, ("dir", "row"), None),
            P("dir", None),
            P("dir"),
            P("dir", None),
            P("dir", None),
            P(),
        ),
        out_specs=(P("dir", "row", None), P(("dir", "row"))),
        check_vma=False,
    )
```

profile of v0, /device:TPU:0, one launch (start us, length us, event | category | flops | bytes accessed | tf_op | source)
XLA Modules:
  0.0 220.8 jit_solution(13710103042672842564)
XLA Ops:
  2.0 2.9 %collective-permute-start = (s32[]{:T(128)}, s32[]{:T(128)}, u32[]{:S(2)}, u32[]{:S(2)}) collective-permute-start(s32[]{:T(128)} %bitcast.24), channel_id=1, source_target_pairs={{0,16},{16,0},{1,17},{17,1},{2,18},{18,2},{3,19},{19,3},{4,20},{20... | collective-permute-start | bytes 20 | tf_op jit(solution)/shard_map/ppermute | solution.py:406
  11.3 21.4 %shard_map.114 = (bf16[2,4,2,256,512]{4,3,2,1,0:T(8,128)(2,1)}, bf16[2,4,2,256,512]{4,3,2,1,0:T(8,128)(2,1)}) custom-call(s32[2]{0:T(128)S(1)} %get-tuple-element.64.spot, bf16[2,256,8192]{2,1,0:T(8,128)(2,1)} %noise.1, f32[256,1]{1,0:T(8,128)S(1)} %fusion.29.rows_squared, f32[1,8192]{1,0:T(1,128)S(1)} %fusion.63.columns_squared, ...), custom_call_target="tpu_custom_call" | custom-call | flops 20000000000 | bytes 20000000 | tf_op jit(solution)/shard_map/pallas_call | solution.py:282
  34.6 6.2 %shard_map.113.matrix = bf16[1024,1024]{1,0:T(8,128)(2,1)} custom-call(f32[2,1024,4]{2,1,0:T(8,128)} %copy.137.slow, f32[2,128,128]{2,1,0:T(8,128)} %constant.332.clone.fast), custom_call_target="tpu_custom_call" | custom-call | flops 8000000 | bytes 4000000 | tf_op jit(solution)/shard_map/pallas_call | solution.py:332
  40.8 2.2 copy-done
  44.6 2.5 %shard_map.115 = bf16[2,512,512]{2,1,0:T(8,128)(2,1)S(1)} custom-call(bf16[1024,1024]{1,0:T(8,128)(2,1)S(1)} %copy-done.2, bf16[2,4,2,256,512]{4,3,2,1,0:T(8,128)(2,1)S(1)} %copy-done, bf16[2,4,2,256,512]{4,3,2,1,0:T(8,128)(2,1)} %collective-permute-done.1.received), custom_call_target="tpu_custom_call" | custom-call | flops 1073741824 | bytes 4000000 | tf_op jit(solution)/shard_map/pallas_call | solution.py:377
  47.1 2.1 collective-permute-start.2
  49.2 2.5 %shard_map.118 = bf16[2,512,512]{2,1,0:T(8,128)(2,1)S(1)} custom-call(bf16[1024,1024]{1,0:T(8,128)(2,1)S(1)} %copy-done.2, bf16[2,4,2,256,512]{4,3,2,1,0:T(8,128)(2,1)S(1)} %copy-done, bf16[2,4,2,256,512]{4,3,2,1,0:T(8,128)(2,1)} %collective-permute-done.1.received), custom_call_target="tpu_custom_call" | custom-call | flops 1073741824 | bytes 4000000 | tf_op jit(solution)/shard_map/pallas_call | solution.py:377
  53.7 3.3 %shard_map.121 = bf16[2,512,512]{2,1,0:T(8,128)(2,1)} custom-call(bf16[1024,1024]{1,0:T(8,128)(2,1)S(1)} %copy-done.2, bf16[2,4,2,256,512]{4,3,2,1,0:T(8,128)(2,1)S(1)} %copy-done, bf16[2,4,2,256,512]{4,3,2,1,0:T(8,128)(2,1)} %collective-permute-done.1.received), custom_call_target="tpu_custom_call" | custom-call | flops 1073741824 | bytes 4000000 | tf_op jit(solution)/shard_map/pallas_call | solution.py:377
  57.0 3.3 %shard_map.124 = bf16[2,512,512]{2,1,0:T(8,128)(2,1)} custom-call(bf16[1024,1024]{1,0:T(8,128)(2,1)S(1)} %copy-done.2, bf16[2,4,2,256,512]{4,3,2,1,0:T(8,128)(2,1)S(1)} %copy-done, bf16[2,4,2,256,512]{4,3,2,1,0:T(8,128)(2,1)} %collective-permute-done.1.received), custom_call_target="tpu_custom_call" | custom-call | flops 1073741824 | bytes 4000000 | tf_op jit(solution)/shard_map/pallas_call | solution.py:377
  60.2 12.8 %collective-permute-done.2 = bf16[2,512,512]{2,1,0:T(8,128)(2,1)S(1)} collective-permute-done((bf16[2,512,512]{2,1,0:T(8,128)(2,1)S(1)}, bf16[2,512,512]{2,1,0:T(8,128)(2,1)S(1)}, u32[]{:S(2)}, u32[]{:S(2)}) %collective-permute-start.2) | collective-permute-done | bytes 1048608 | tf_op jit(solution)/shard_map/ppermute | solution.py:421
  73.1 2.6 %shard_map.116 = bf16[1,512,512]{2,1,0:T(8,128)(2,1)} custom-call(bf16[1024,1024]{1,0:T(8,128)(2,1)S(1)} %copy-done.2, bf16[2,4,2,256,512]{4,3,2,1,0:T(8,128)(2,1)S(1)} %copy-done, bf16[2,4,2,256,512]{4,3,2,1,0:T(8,128)(2,1)} %collective-permute-done.1.received, bf16[1,512,512]{2,1,0:T(8,128)(2,1)S(1)} %get-tuple-element.31.rest_0_), custom_call_target="tpu_custom_call" | custom-call | flops 536870912 | bytes 4000000 | tf_op jit(solution)/shard_map/pallas_call | solution.py:377
  79.0 2.7 %shard_map.119 = bf16[1,512,512]{2,1,0:T(8,128)(2,1)} custom-call(bf16[1024,1024]{1,0:T(8,128)(2,1)S(1)} %copy-done.2, bf16[2,4,2,256,512]{4,3,2,1,0:T(8,128)(2,1)S(1)} %copy-done, bf16[2,4,2,256,512]{4,3,2,1,0:T(8,128)(2,1)} %collective-permute-done.1.received, bf16[1,512,512]{2,1,0:T(8,128)(2,1)S(1)} %get-tuple-element.33.rest_0_), custom_call_target="tpu_custom_call" | custom-call | flops 536870912 | bytes 4000000 | tf_op jit(solution)/shard_map/pallas_call | solution.py:377
  84.2 6.5 %collective-permute-done.3.rest_1_ = bf16[1,512,512]{2,1,0:T(8,128)(2,1)} collective-permute-done((bf16[1,512,512]{2,1,0:T(8,128)(2,1)}, bf16[1,512,512]{2,1,0:T(8,128)(2,1)}, u32[]{:S(2)}, u32[]{:S(2)}) %collective-permute-start.3) | collective-permute-done | bytes 524320 | tf_op jit(solution)/shard_map/ppermute | solution.py:422
  90.7 2.2 copy-done.1
  92.9 1.9 shard_map.117
  95.0 1.9 collective-permute-start.4
  96.8 2.6 %collective-permute-start.5 = (bf16[512,128]{1,0:T(8,128)(2,1)S(1)}, bf16[512,128]{1,0:T(8,128)(2,1)S(1)}, u32[]{:S(2)}, u32[]{:S(2)}) collective-permute-start(bf16[512,128]{1,0:T(8,128)(2,1)S(1)} %get-tuple-element.41), channel_id=1, source_target_pairs={{0,8},{1,9},{2,10},{3,11},{4,12},{5,13},{6,14},{7,15},{8,0},{9,1},... | collective-permute-start | bytes 393224 | tf_op jit(solution)/shard_map/ppermute | solution.py:448
  99.4 14.0 %collective-permute-done.8.rest_1_ = bf16[1,512,512]{2,1,0:T(8,128)(2,1)} collective-permute-done((bf16[1,512,512]{2,1,0:T(8,128)(2,1)}, bf16[1,512,512]{2,1,0:T(8,128)(2,1)}, u32[]{:S(2)}, u32[]{:S(2)}) %collective-permute-start.8) | collective-permute-done | bytes 524320 | tf_op jit(solution)/shard_map/ppermute | solution.py:421
  113.4 3.6 %collective-permute-start.6 = (bf16[512,128]{1,0:T(8,128)(2,1)S(1)}, bf16[512,128]{1,0:T(8,128)(2,1)S(1)}, u32[]{:S(2)}, u32[]{:S(2)}) collective-permute-start(bf16[512,128]{1,0:T(8,128)(2,1)S(1)} %get-tuple-element.40), channel_id=1, source_target_pairs={{0,12},{1,13},{2,14},{3,15},{4,8},{5,9},{6,10},{7,11},{8,4},{9,5},... | collective-permute-start | bytes 393224 | tf_op jit(solution)/shard_map/ppermute | solution.py:448
  117.1 1.9 shard_map.120
  125.8 2.0 collective-permute-start.11
  136.8 2.2 collective-permute-start.15
  140.7 1.8 shard_map.126
  142.9 2.4 %collective-permute-start.20 = (bf16[512,128]{1,0:T(8,128)(2,1)S(1)}, bf16[512,128]{1,0:T(8,128)(2,1)S(1)}, u32[]{:S(2)}, u32[]{:S(2)}) collective-permute-start(bf16[512,128]{1,0:T(8,128)(2,1)S(1)} %get-tuple-element.50), channel_id=1, source_target_pairs={{0,8},{1,9},{2,10},{3,11},{4,12},{5,13},{6,14},{7,15},{8,0},{9,1},... | collective-permute-start | bytes 393224 | tf_op jit(solution)/shard_map/ppermute | solution.py:448
  145.3 2.6 %collective-permute-start.21 = (bf16[512,128]{1,0:T(8,128)(2,1)S(1)}, bf16[512,128]{1,0:T(8,128)(2,1)S(1)}, u32[]{:S(2)}, u32[]{:S(2)}) collective-permute-start(bf16[512,128]{1,0:T(8,128)(2,1)S(1)} %get-tuple-element.49), channel_id=1, source_target_pairs={{0,12},{1,13},{2,14},{3,15},{4,8},{5,9},{6,10},{7,11},{8,4},{9,5},... | collective-permute-start | bytes 393224 | tf_op jit(solution)/shard_map/ppermute | solution.py:448
  148.0 2.5 %collective-permute-done.16 = bf16[512,128]{1,0:T(8,128)(2,1)S(1)} collective-permute-done((bf16[512,128]{1,0:T(8,128)(2,1)S(1)}, bf16[512,128]{1,0:T(8,128)(2,1)S(1)}, u32[]{:S(2)}, u32[]{:S(2)}) %collective-permute-start.16) | collective-permute-done | bytes 131104 | tf_op jit(solution)/shard_map/ppermute | solution.py:448
  150.7 8.4 %collective-permute-done.20 = bf16[512,128]{1,0:T(8,128)(2,1)S(1)} collective-permute-done((bf16[512,128]{1,0:T(8,128)(2,1)S(1)}, bf16[512,128]{1,0:T(8,128)(2,1)S(1)}, u32[]{:S(2)}, u32[]{:S(2)}) %collective-permute-start.20) | collective-permute-done | bytes 131104 | tf_op jit(solution)/shard_map/ppermute | solution.py:448
  159.3 4.0 %cosine_convert_fusion = (bf16[1,16,32,512]{3,1,0,2:T(8,128)(2,1)S(1)}, bf16[1,16,32,512]{3,1,0,2:T(8,128)(2,1)S(1)}) fusion(f32[1,16,32,128]{3,1,0,2:T(8,128)S(1)} %copy.141, f32[1,16,32,128]{3,1,0,2:T(8,128)S(1)} %copy.140, f32[1,16,32,128]{3,1,0,2:T(8,128)S(1)} %copy.139, f32[1,16,32,128]{3,1,0,2:T(8,128)S(1)} %copy.138, f32[]{:T(128)S(6)} %add.566), kind=kLoop, calls=%fused_computation.54 | loop fusion | flops 1572864 | bytes 2097156 | tf_op jit(solution)/shard_map/convert.16
  170.2 4.4 %all-to-all-start = ((bf16[2,16,32,512]{3,2,0,1:T(8,128)(2,1)}), bf16[2,16,32,512]{3,2,0,1:T(8,128)(2,1)S(1)}, u32[]{:S(2)}, u32[]{:S(2)}) async-start(bf16[2,16,32,512]{3,2,0,1:T(8,128)(2,1)} %copy.151), calls=%async_computation | async-start | bytes 2097152 | tf_op jit(solution)/shard_map/all_to_all | solution.py:472
  176.7 20.8 %all-to-all-done = bf16[2,16,32,512]{3,2,0,1:T(8,128)(2,1)S(1)} async-done(((bf16[2,16,32,512]{3,2,0,1:T(8,128)(2,1)}), bf16[2,16,32,512]{3,2,0,1:T(8,128)(2,1)S(1)}, u32[]{:S(2)}, u32[]{:S(2)}) %all-to-all-start) | async-done | bytes 1048608 | tf_op jit(solution)/shard_map/all_to_all | solution.py:472
  203.8 2.3 %gather_fusion = f32[512]{0:T(512)S(1)} fusion(f32[1024]{0:T(1024)S(1)} %multiply_bitcast_fusion, s32[1024]{0:T(1024)S(1)} %pad_clamp_fusion), kind=kCustom, calls=%fused_computation | custom fusion | bytes 6144 | tf_op jit(solution)/shard_map/jit(_take)/gather | solution.py:489
  206.3 13.9 %all_to_all.20 = f32[32,2,16]{2,1,0:T(2,128)S(1)} all-to-all(f32[32,2,16]{2,1,0:T(2,128)S(1)} %copy.160), channel_id=1, replica_groups=mesh['dir'=2,'row'=16] {'dir','row'}, dimensions={0} | all-to-all | bytes 8192 | tf_op jit(solution)/shard_map/all_to_all | solution.py:497
  (139 shorter events, 51.1 us)
Async XLA Ops:
  2.0 4.5 %collective-permute-start = (s32[]{:T(128)}, s32[]{:T(128)}, u32[]{:S(2)}, u32[]{:S(2)}) collective-permute-start(s32[]{:T(128)} %bitcast.24), channel_id=1, source_target_pairs={{0,16},{16,0},{1,17},{17,1},{2,18},{18,2},{3,19},{19,3},{4,20},{20... | collective-permute-start | bytes 20 | tf_op jit(solution)/shard_map/ppermute | solution.py:406
  7.8 1.6 copy-start.4
  32.7 8.0 %collective-permute-start.1 = (bf16[2,4,2,256,512]{4,3,2,1,0:T(8,128)(2,1)}, bf16[2,4,2,256,512]{4,3,2,1,0:T(8,128)(2,1)}, u32[]{:S(2)}, u32[]{:S(2)}) collective-permute-start(bf16[2,4,2,256,512]{4,3,2,1,0:T(8,128)(2,1)} %get-tuple-element.7), channel_id=1, source_target_pairs={{0,1},{1,0},{2,3},{3,2},{4,5},{5,4},{6,7},{7,6},{8,9},{9,8},{10,11... | collective-permute-start | bytes 12582920 | tf_op jit(solution)/shard_map/ppermute | solution.py:408
  40.8 2.2 copy-start
  43.0 1.6 copy-start.2
  47.1 25.9 %collective-permute-start.2 = (bf16[2,512,512]{2,1,0:T(8,128)(2,1)S(1)}, bf16[2,512,512]{2,1,0:T(8,128)(2,1)S(1)}, u32[]{:S(2)}, u32[]{:S(2)}) collective-permute-start(bf16[2,512,512]{2,1,0:T(8,128)(2,1)S(1)} %shard_map.115), channel_id=1, source_target_pairs={{0,16},{16,0},{1,17},{17,1},{2,18},{18,2},{3,19},{19,3},{4,20},{20... | collective-permute-start | bytes 3145736 | tf_op jit(solution)/shard_map/ppermute | solution.py:421
  51.7 27.2 %collective-permute-start.7 = (bf16[2,512,512]{2,1,0:T(8,128)(2,1)S(1)}, bf16[2,512,512]{2,1,0:T(8,128)(2,1)S(1)}, u32[]{:S(2)}, u32[]{:S(2)}) collective-permute-start(bf16[2,512,512]{2,1,0:T(8,128)(2,1)S(1)} %shard_map.118), channel_id=1, source_target_pairs={{0,2},{1,3},{2,0},{3,1},{4,6},{5,7},{6,4},{7,5},{8,10},{9,11},{10,... | collective-permute-start | bytes 3145736 | tf_op jit(solution)/shard_map/ppermute | solution.py:422
  75.6 15.1 %collective-permute-start.3 = (bf16[1,512,512]{2,1,0:T(8,128)(2,1)}, bf16[1,512,512]{2,1,0:T(8,128)(2,1)}, u32[]{:S(2)}, u32[]{:S(2)}) collective-permute-start(bf16[1,512,512]{2,1,0:T(8,128)(2,1)} %shard_map.116), channel_id=1, source_target_pairs={{0,2},{1,3},{2,0},{3,1},{4,6},{5,7},{6,4},{7,5},{8,10},{9,11},{10,... | collective-permute-start | bytes 1572872 | tf_op jit(solution)/shard_map/ppermute | solution.py:422
  77.4 41.7 %collective-permute-start.12 = (bf16[2,512,512]{2,1,0:T(8,128)(2,1)}, bf16[2,512,512]{2,1,0:T(8,128)(2,1)}, u32[]{:S(2)}, u32[]{:S(2)}) collective-permute-start(bf16[2,512,512]{2,1,0:T(8,128)(2,1)} %shard_map.121), channel_id=1, source_target_pairs={{0,16},{16,0},{1,17},{17,1},{2,18},{18,2},{3,19},{19,3},{4,20},{20... | collective-permute-start | bytes 3145736 | tf_op jit(solution)/shard_map/ppermute | solution.py:421
  79.0 11.8 %copy-start.3 = (bf16[1024,1024]{1,0:T(8,128)(2,1)S(1)}, bf16[1024,1024]{1,0:T(8,128)(2,1)}, u32[]{:S(2)}) copy-start(bf16[1024,1024]{1,0:T(8,128)(2,1)} %shard_map.113.matrix) | copy-start | bytes 6291460
  81.7 31.8 %collective-permute-start.8 = (bf16[1,512,512]{2,1,0:T(8,128)(2,1)}, bf16[1,512,512]{2,1,0:T(8,128)(2,1)}, u32[]{:S(2)}, u32[]{:S(2)}) collective-permute-start(bf16[1,512,512]{2,1,0:T(8,128)(2,1)} %shard_map.119), channel_id=1, source_target_pairs={{0,16},{16,0},{1,17},{17,1},{2,18},{18,2},{3,19},{19,3},{4,20},{20... | collective-permute-start | bytes 1572872 | tf_op jit(solution)/shard_map/ppermute | solution.py:421
  82.2 40.0 %collective-permute-start.17 = (bf16[2,512,512]{2,1,0:T(8,128)(2,1)}, bf16[2,512,512]{2,1,0:T(8,128)(2,1)}, u32[]{:S(2)}, u32[]{:S(2)}) collective-permute-start(bf16[2,512,512]{2,1,0:T(8,128)(2,1)} %shard_map.124), channel_id=1, source_target_pairs={{0,2},{1,3},{2,0},{3,1},{4,6},{5,7},{6,4},{7,5},{8,10},{9,11},{10,... | collective-permute-start | bytes 3145736 | tf_op jit(solution)/shard_map/ppermute | solution.py:422
  90.7 2.2 copy-start.1
  95.0 30.8 %collective-permute-start.4 = (bf16[512,128]{1,0:T(8,128)(2,1)S(1)}, bf16[512,128]{1,0:T(8,128)(2,1)S(1)}, u32[]{:S(2)}, u32[]{:S(2)}) collective-permute-start(bf16[512,128]{1,0:T(8,128)(2,1)S(1)} %get-tuple-element.39), channel_id=1, source_target_pairs={{0,4},{1,5},{2,6},{3,7},{4,0},{5,1},{6,2},{7,3},{8,12},{9,13},{10,... | collective-permute-start | bytes 393224 | tf_op jit(solution)/shard_map/ppermute | solution.py:448
  96.8 31.0 %collective-permute-start.5 = (bf16[512,128]{1,0:T(8,128)(2,1)S(1)}, bf16[512,128]{1,0:T(8,128)(2,1)S(1)}, u32[]{:S(2)}, u32[]{:S(2)}) collective-permute-start(bf16[512,128]{1,0:T(8,128)(2,1)S(1)} %get-tuple-element.41), channel_id=1, source_target_pairs={{0,8},{1,9},{2,10},{3,11},{4,12},{5,13},{6,14},{7,15},{8,0},{9,1},... | collective-permute-start | bytes 393224 | tf_op jit(solution)/shard_map/ppermute | solution.py:448
  113.4 15.9 %collective-permute-start.6 = (bf16[512,128]{1,0:T(8,128)(2,1)S(1)}, bf16[512,128]{1,0:T(8,128)(2,1)S(1)}, u32[]{:S(2)}, u32[]{:S(2)}) collective-permute-start(bf16[512,128]{1,0:T(8,128)(2,1)S(1)} %get-tuple-element.40), channel_id=1, source_target_pairs={{0,12},{1,13},{2,14},{3,15},{4,8},{5,9},{6,10},{7,11},{8,4},{9,5},... | collective-permute-start | bytes 393224 | tf_op jit(solution)/shard_map/ppermute | solution.py:448
  119.1 11.9 %collective-permute-start.10 = (bf16[512,128]{1,0:T(8,128)(2,1)S(1)}, bf16[512,128]{1,0:T(8,128)(2,1)S(1)}, u32[]{:S(2)}, u32[]{:S(2)}) collective-permute-start(bf16[512,128]{1,0:T(8,128)(2,1)S(1)} %get-tuple-element.44), channel_id=1, source_target_pairs={{0,8},{1,9},{2,10},{3,11},{4,12},{5,13},{6,14},{7,15},{8,0},{9,1},... | collective-permute-start | bytes 393224 | tf_op jit(solution)/shard_map/ppermute | solution.py:448
  122.2 12.1 %collective-permute-start.13 = (bf16[1,512,512]{2,1,0:T(8,128)(2,1)S(1)}, bf16[1,512,512]{2,1,0:T(8,128)(2,1)S(1)}, u32[]{:S(2)}, u32[]{:S(2)}) collective-permute-start(bf16[1,512,512]{2,1,0:T(8,128)(2,1)S(1)} %shard_map.122), channel_id=1, source_target_pairs={{0,2},{1,3},{2,0},{3,1},{4,6},{5,7},{6,4},{7,5},{8,10},{9,11},{10,... | collective-permute-start | bytes 1572872 | tf_op jit(solution)/shard_map/ppermute | solution.py:422
  125.8 7.0 %collective-permute-start.11 = (bf16[512,128]{1,0:T(8,128)(2,1)S(1)}, bf16[512,128]{1,0:T(8,128)(2,1)S(1)}, u32[]{:S(2)}, u32[]{:S(2)}) collective-permute-start(bf16[512,128]{1,0:T(8,128)(2,1)S(1)} %get-tuple-element.43), channel_id=1, source_target_pairs={{0,12},{1,13},{2,14},{3,15},{4,8},{5,9},{6,10},{7,11},{8,4},{9,5},... | collective-permute-start | bytes 393224 | tf_op jit(solution)/shard_map/ppermute | solution.py:448
  127.8 6.3 %collective-permute-start.9 = (bf16[512,128]{1,0:T(8,128)(2,1)S(1)}, bf16[512,128]{1,0:T(8,128)(2,1)S(1)}, u32[]{:S(2)}, u32[]{:S(2)}) collective-permute-start(bf16[512,128]{1,0:T(8,128)(2,1)S(1)} %get-tuple-element.42), channel_id=1, source_target_pairs={{0,4},{1,5},{2,6},{3,7},{4,0},{5,1},{6,2},{7,3},{8,12},{9,13},{10,... | collective-permute-start | bytes 393224 | tf_op jit(solution)/shard_map/ppermute | solution.py:448
  129.3 11.4 %collective-permute-start.18 = (bf16[1,512,512]{2,1,0:T(8,128)(2,1)S(1)}, bf16[1,512,512]{2,1,0:T(8,128)(2,1)S(1)}, u32[]{:S(2)}, u32[]{:S(2)}) collective-permute-start(bf16[1,512,512]{2,1,0:T(8,128)(2,1)S(1)} %shard_map.125), channel_id=1, source_target_pairs={{0,16},{16,0},{1,17},{17,1},{2,18},{18,2},{3,19},{19,3},{4,20},{20... | collective-permute-start | bytes 1572872 | tf_op jit(solution)/shard_map/ppermute | solution.py:421
  136.2 9.1 %collective-permute-start.14 = (bf16[512,128]{1,0:T(8,128)(2,1)S(1)}, bf16[512,128]{1,0:T(8,128)(2,1)S(1)}, u32[]{:S(2)}, u32[]{:S(2)}) collective-permute-start(bf16[512,128]{1,0:T(8,128)(2,1)S(1)} %get-tuple-element.45), channel_id=1, source_target_pairs={{0,4},{1,5},{2,6},{3,7},{4,0},{5,1},{6,2},{7,3},{8,12},{9,13},{10,... | collective-permute-start | bytes 393224 | tf_op jit(solution)/shard_map/ppermute | solution.py:448
  136.8 11.1 %collective-permute-start.15 = (bf16[512,128]{1,0:T(8,128)(2,1)S(1)}, bf16[512,128]{1,0:T(8,128)(2,1)S(1)}, u32[]{:S(2)}, u32[]{:S(2)}) collective-permute-start(bf16[512,128]{1,0:T(8,128)(2,1)S(1)} %get-tuple-element.47), channel_id=1, source_target_pairs={{0,8},{1,9},{2,10},{3,11},{4,12},{5,13},{6,14},{7,15},{8,0},{9,1},... | collective-permute-start | bytes 393224 | tf_op jit(solution)/shard_map/ppermute | solution.py:448
  139.0 11.4 %collective-permute-start.16 = (bf16[512,128]{1,0:T(8,128)(2,1)S(1)}, bf16[512,128]{1,0:T(8,128)(2,1)S(1)}, u32[]{:S(2)}, u32[]{:S(2)}) collective-permute-start(bf16[512,128]{1,0:T(8,128)(2,1)S(1)} %get-tuple-element.46), channel_id=1, source_target_pairs={{0,12},{1,13},{2,14},{3,15},{4,8},{5,9},{6,10},{7,11},{8,4},{9,5},... | collective-permute-start | bytes 393224 | tf_op jit(solution)/shard_map/ppermute | solution.py:448
  142.5 8.1 %collective-permute-start.19 = (bf16[512,128]{1,0:T(8,128)(2,1)S(1)}, bf16[512,128]{1,0:T(8,128)(2,1)S(1)}, u32[]{:S(2)}, u32[]{:S(2)}) collective-permute-start(bf16[512,128]{1,0:T(8,128)(2,1)S(1)} %get-tuple-element.48), channel_id=1, source_target_pairs={{0,4},{1,5},{2,6},{3,7},{4,0},{5,1},{6,2},{7,3},{8,12},{9,13},{10,... | collective-permute-start | bytes 393224 | tf_op jit(solution)/shard_map/ppermute | solution.py:448
  142.9 16.2 %collective-permute-start.20 = (bf16[512,128]{1,0:T(8,128)(2,1)S(1)}, bf16[512,128]{1,0:T(8,128)(2,1)S(1)}, u32[]{:S(2)}, u32[]{:S(2)}) collective-permute-start(bf16[512,128]{1,0:T(8,128)(2,1)S(1)} %get-tuple-element.50), channel_id=1, source_target_pairs={{0,8},{1,9},{2,10},{3,11},{4,12},{5,13},{6,14},{7,15},{8,0},{9,1},... | collective-permute-start | bytes 393224 | tf_op jit(solution)/shard_map/ppermute | solution.py:448
  145.3 13.8 %collective-permute-start.21 = (bf16[512,128]{1,0:T(8,128)(2,1)S(1)}, bf16[512,128]{1,0:T(8,128)(2,1)S(1)}, u32[]{:S(2)}, u32[]{:S(2)}) collective-permute-start(bf16[512,128]{1,0:T(8,128)(2,1)S(1)} %get-tuple-element.49), channel_id=1, source_target_pairs={{0,12},{1,13},{2,14},{3,15},{4,8},{5,9},{6,10},{7,11},{8,4},{9,5},... | collective-permute-start | bytes 393224 | tf_op jit(solution)/shard_map/ppermute | solution.py:448
  168.6 6.7 %copy-start.7 = (s32[1,512]{1,0:T(1,128)S(1)}, s32[1,512]{1,0:T(1,128)}, u32[]{:S(2)}) copy-start(s32[1,512]{1,0:T(1,128)} %param.13) | copy-start | bytes 6148
  170.2 27.4 %all-to-all-start = ((bf16[2,16,32,512]{3,2,0,1:T(8,128)(2,1)}), bf16[2,16,32,512]{3,2,0,1:T(8,128)(2,1)S(1)}, u32[]{:S(2)}, u32[]{:S(2)}) async-start(bf16[2,16,32,512]{3,2,0,1:T(8,128)(2,1)} %copy.151), calls=%async_computation | async-start | bytes 2097152 | tf_op jit(solution)/shard_map/all_to_all | solution.py:472
  202.2 3.9 %copy-start.9 = (f32[1,512]{1,0:T(1,128)S(1)}, f32[1,512]{1,0:T(1,128)}, u32[]{:S(2)}) copy-start(f32[1,512]{1,0:T(1,128)} %param.14) | copy-start | bytes 6148
  202.2 3.9 %copy-start.10 = (s32[512]{0:T(512)S(1)}, s32[512]{0:T(512)}, u32[]{:S(2)}) copy-start(s32[512]{0:T(512)} %param.15) | copy-start | bytes 6148
  203.7 17.1 %copy-start.8 = (f32[8,128]{1,0:T(8,128)}, f32[8,128]{1,0:T(8,128)S(1)}, u32[]{:S(2)}) copy-start(f32[8,128]{1,0:T(8,128)S(1)} %fusion.2) | copy-start | bytes 12292
  (2 other events, 1.9 us)
where the time goes:
time: 222 us; the launch traced here: 221 us
  waiting for transfers between devices  69.4 us (31%)
  Pallas kernels  55.3 us (25%)
  starting transfers between devices  38.6 us (17%)
  local copies, waits for them, and re-layouts  23 us (10%)
  blocking collectives  13.9 us (6%)
  other arithmetic  12.3 us (6%)
  matrix products  5.08 us (2%)
  between operations  3.23 us (1%)
    pallas_call x12, Pallas kernels, patch_product(): pl.pallas_call(product_kernel, grid=(bin_count, side_count), in_specs=[pl...  27.7 us
    ppermute x4, waiting for transfers between devices, over(): return lax.ppermute(values, 'dir', over_x)  26.8 us
    ppermute x12, starting transfers between devices, reduced_patch(): sent = lax.ppermute(slice_for(z_spot ^ shift), 'row', pairs)  21.5 us
    pallas_call x1, Pallas kernels, half_screens(): pl.pallas_call(screen_kernel, grid=(rows_here // step,), in_specs=[pl.Blo...  21.4 us
    all_to_all x1, waiting for transfers between devices, body(): lax.all_to_all(stacked_field, 'row', split_axis=1, concat_axis=3, tiled=T...  20.8 us
    ppermute x12, waiting for transfers between devices, reduced_patch(): sent = lax.ppermute(slice_for(z_spot ^ shift), 'row', pairs)  14 us
    all_to_all x1, blocking collectives, body(): lax.all_to_all(terms.transpose(1, 0, 2), ('dir', 'row'), split_axis=0, co...  13.9 us
    unnamed x22, local copies, waits for them, and re-layouts  9.53 us
  transfers between devices with their start and end apart: 23, of which 9 were waited for; matrix products, arithmetic and copies ran while one was open for 4% of the time, Pallas kernels for 14%

commit v1 on v0

--- a/solution.py
+++ b/solution.py
@@ -344,111 +344,189 @@
     )(slow, fast)
 
 
-def product_kernel(matrix, kept, received, *rest):
-    *added, result = rest
+def product_kernel(matrix, kept, received, result):
     depth = kept.shape[0] * kept.shape[1]
+    columns = kept.shape[2]
     total = jnp.dot(
         matrix[:, :depth],
-        kept[...].reshape(depth, kept.shape[2]),
+        kept[...].reshape(depth, columns),
         preferred_element_type=jnp.float32,
     )
     total += jnp.dot(
         matrix[:, depth:],
-        received[...].reshape(depth, kept.shape[2]),
+        received[...].reshape(depth, columns),
         preferred_element_type=jnp.float32,
     )
-    for term in added:
-        total += term[...].astype(jnp.float32)
-    result[...] = total.astype(result.dtype)
-
-
-def patch_product(matrix, bins, kept, received, sides, chunk, *added):
+    result[...] = total.astype(result.dtype).reshape(result.shape)
+
+
+def patch_products(matrix, kept, received):
     patch_len = matrix.shape[0] // 2
-    _, _, parts, rows, columns = kept.shape
-    bin_start, bin_count = bins
-    side_start, side_count = sides
+    sides, chunks, parts, rows, columns = kept.shape
     values_spec = pl.BlockSpec(
-        (None, None, parts, rows, columns), lambda i, j: (side_start + j, chunk, 0, 0, 0)
-    )
-    result_spec = pl.BlockSpec(
-        (None, patch_len, columns), lambda i, j: (i * side_count + j, 0, 0)
-    )
-    count = bin_count * side_count
+        (None, None, parts, rows, columns), lambda i, j: (j, i, 0, 0, 0)
+    )
     return pl.pallas_call(
         product_kernel,
-        grid=(bin_count, side_count),
+        grid=(chunks, sides),
         in_specs=[
-            pl.BlockSpec((patch_len, matrix.shape[1]), lambda i, j: (bin_start + i, 0)),
+            pl.BlockSpec(matrix.shape, lambda i, j: (0, 0)),
             values_spec,
             values_spec,
-        ]
-        + [result_spec] * len(added),
-        out_specs=result_spec,
-        out_shape=jax.ShapeDtypeStruct((count, patch_len, columns), jnp.bfloat16),
+        ],
+        out_specs=pl.BlockSpec(
+            (None, 2, None, patch_len, columns), lambda i, j: (i, 0, j, 0, 0)
+        ),
+        out_shape=jax.ShapeDtypeStruct((chunks, 2, sides, patch_len, columns), jnp.bfloat16),
         compiler_params=pltpu.CompilerParams(vmem_limit_bytes=32 * 1024 * 1024),
         cost_estimate=pl.CostEstimate(
-            flops=2 * count * patch_len * matrix.shape[1] * columns,
-            bytes_accessed=4_000_000,
-            transcendentals=0,
+            flops=9_000_000_000, bytes_accessed=20_000_000, transcendentals=0
         ),
-    )(matrix, kept, received, *added)
+    )(matrix, kept, received)
+
+
+def reduce_kernel(
+    products, result, a_recv, b_send, b_recv, z_send, z_recv, a_sems, b_sems, z_sems
+):
+    here_x, row = (lax.axis_index("dir"), lax.axis_index("row"))
+    z_spot, y_spot = (row // 4, row // 2 % 2)
+    x_mate = (1 - here_x, row)
+    y_mate = (here_x, row + 2 - 4 * y_spot)
+    z_spots = [(z_spot + shift) % 4 for shift in range(1, 4)]
+    z_mates = [(here_x, row + 4 * (spot - z_spot)) for spot in z_spots]
+    mates = [x_mate, y_mate] + z_mates
+    barrier = pltpu.get_barrier_semaphore()
+    for mate in mates:
+        pl.semaphore_signal(barrier, inc=1, device_id=mate, device_id_type=pl.DeviceIdType.MESH)
+    pl.semaphore_wait(barrier, len(mates))
+
+    height = a_recv.shape[2]
+    units = [
+        (2 * pair + way, half) for pair in range(2) for half in range(2) for way in range(2)
+    ]
+
+    def copy(source, target, sems, spot, mate):
+        return pltpu.make_async_remote_copy(
+            src_ref=source,
+            dst_ref=target,
+            send_sem=sems.at[(0, *spot)],
+            recv_sem=sems.at[(1, *spot)],
+            device_id=mate,
+            device_id_type=pl.DeviceIdType.MESH,
+        )
+
+    def rows_of(unit):
+        return pl.ds(units[unit][1] * height, height)
+
+    a_copies, b_copies, z_copies = ([], [], [])
+    for unit, (chunk, _) in enumerate(units):
+        rows = rows_of(unit)
+        if chunk % 2 == 0:
+            source = products.at[chunk, 1, :, rows, :]
+            first_mate, second_mate = (x_mate, y_mate)
+        else:
+            source = products.at[chunk, :, 1, rows, :]
+            first_mate, second_mate = (y_mate, x_mate)
+        a_copies.append(copy(source, a_recv.at[unit], a_sems, (unit,), first_mate))
+        b_copies.append(copy(b_send.at[unit], b_recv.at[unit], b_sems, (unit,), second_mate))
+        z_copies.append(
+            [
+                copy(
+                    z_send.at[unit, z_spots[shift]],
+                    z_recv.at[unit, shift],
+                    z_sems,
+                    (unit, shift),
+                    z_mates[shift],
+                )
+                for shift in range(3)
+            ]
+        )
+
+    def finish(unit):
+        chunk, _ = units[unit]
+        b_copies[unit].wait_recv()
+        total = (
+            products[chunk, 0, 0, rows_of(unit), :].astype(jnp.float32)
+            + a_recv[unit, 0].astype(jnp.float32)
+            + b_recv[unit].astype(jnp.float32)
+        ).astype(jnp.bfloat16)
+        for spot in range(4):
+            z_send[unit, spot] = total[:, spot * SECOND : (spot + 1) * SECOND]
+        for sent in z_copies[unit]:
+            sent.start()
+
+    count = len(units)
+    ahead = 4
+    for unit in range(ahead):
+        a_copies[unit].start()
+    for unit, (chunk, _) in enumerate(units):
+        a_copies[unit].wait_recv()
+        side = (0, 1) if chunk % 2 == 0 else (1, 0)
+        b_send[unit] = (
+            products[chunk, side[0], side[1], rows_of(unit), :].astype(jnp.float32)
+            + a_recv[unit, 1].astype(jnp.float32)
+        ).astype(jnp.bfloat16)
+        b_copies[unit].start()
+        if unit + ahead < count:
+            a_copies[unit + ahead].start()
+        if unit >= 2:
+            finish(unit - 2)
+    finish(count - 2)
+    finish(count - 1)
+    for unit, (chunk, _) in enumerate(units):
+        total = z_send[unit, z_spot].astype(jnp.float32)
+        for shift in range(3):
+            z_copies[unit][shift].wait_recv()
+            total += z_recv[unit, shift].astype(jnp.float32)
+        result[rows_of(unit), chunk * SECOND : (chunk + 1) * SECOND] = total
+    for unit in range(count):
+        a_copies[unit].wait_send()
+        b_copies[unit].wait_send()
+        for sent in z_copies[unit]:
+            sent.wait_send()
+
+
+def reduce_products(products):
+    chunks, _, _, patch_len, columns = products.shape
+    count, height = (2 * chunks, patch_len // 2)
+    held = jnp.bfloat16
+    return pl.pallas_call(
+        reduce_kernel,
+        in_specs=[pl.BlockSpec(memory_space=pltpu.VMEM)],
+        out_specs=pl.BlockSpec(memory_space=pltpu.VMEM),
+        out_shape=jax.ShapeDtypeStruct((patch_len, chunks * SECOND), jnp.float32),
+        scratch_shapes=[
+            pltpu.VMEM((count, 2, height, columns), held),
+            pltpu.VMEM((count, height, columns), held),
+            pltpu.VMEM((count, height, columns), held),
+            pltpu.VMEM((count, 4, height, SECOND), held),
+            pltpu.VMEM((count, 3, height, SECOND), held),
+            pltpu.SemaphoreType.DMA((2, count)),
+            pltpu.SemaphoreType.DMA((2, count)),
+            pltpu.SemaphoreType.DMA((2, count, 3)),
+        ],
+        compiler_params=pltpu.CompilerParams(
+            collective_id=0, has_side_effects=True, vmem_limit_bytes=40 * 1024 * 1024
+        ),
+    )(products)
 
 
 def reduced_patch(white_noise, row_start, geometry):
     row_count = lax.axis_size("row")
     patch_len = row_count * ROWS_DEV
     row = lax.axis_index("row")
-    z_spot = row // 4
     over_core = [(r, r ^ 1) for r in range(row_count)]
-    over_y = [(r, r ^ 2) for r in range(row_count)]
-    over_x = [(0, 1), (1, 0)]
     host = host_tables()
-    other_bin = lax.ppermute(geometry[0, 1], "dir", over_x)
     kept, moved = half_screens(white_noise, row_start, row, host)
     received = lax.ppermute(moved, "row", over_core)
+    slant_bin, kept = lax.optimization_barrier((geometry[0, 1], kept))
+    other_bin = lax.ppermute(slant_bin, "dir", [(0, 1), (1, 0)])
     first_block = 2 * (lax.axis_index("dir") * row_count + row)
     other_block = 2 * (lax.axis_index("dir") * row_count + (row ^ 1))
     block_ids = jnp.stack([first_block, first_block + 1, other_block, other_block + 1])
-    slant_bins = jnp.stack([geometry[0, 1], other_bin])
+    slant_bins = jnp.stack([slant_bin, other_bin])
     matrix = patch_matrix(slant_bins, block_ids, patch_len // SECOND, host[3])
-    own, other, both = ((0, 1), (1, 1), (0, 2))
-
-    def product(bins, sides, chunk, *added):
-        return patch_product(matrix, bins, kept, received, sides, chunk, *added)
-
-    def over(first_x, values):
-        if first_x:
-            return lax.ppermute(values, "dir", over_x)
-        return lax.ppermute(values, "row", over_y)
-
-    arrived = {}
-    for chunk in range(CHUNKS):
-        first_x = chunk % 2 == 0
-        leaving = product(other, both, chunk) if first_x else product(both, other, chunk)
-        if chunk >= 2:
-            leaving, _ = lax.optimization_barrier((leaving, arrived[chunk - 2]))
-        arrived[chunk] = over(first_x, leaving)
-    totals = []
-    for chunk in range(CHUNKS):
-        first_x = chunk % 2 == 0
-        first_kept, first_moved = (arrived[chunk][:1], arrived[chunk][1:])
-        if first_x:
-            second = product(own, other, chunk, first_moved)
-        else:
-            second = product(other, own, chunk, first_moved)
-        second = over(not first_x, second)
-        total = product(own, own, chunk, first_kept, second)[0]
-
-        def slice_for(spot):
-            return lax.dynamic_slice_in_dim(total, spot * SECOND, SECOND, 1)
-
-        result = slice_for(z_spot).astype(jnp.float32)
-        for shift in range(1, 4):
-            pairs = [(r, r ^ (4 * shift)) for r in range(row_count)]
-            sent = lax.ppermute(slice_for(z_spot ^ shift), "row", pairs)
-            result = result + sent.astype(jnp.float32)
-        totals.append(result)
-    return jnp.concatenate(totals, axis=1)
+    return reduce_products(patch_products(matrix, kept, received))
 
 
 def body(white_noise, geometry, window, tile_map, link_gain, serving):

time: 222 us -> 211 us (0.950)
  Pallas kernels: 55.3 us -> 130 us
  waiting for transfers between devices: 69.4 us -> 20.8 us
  starting transfers between devices: 38.6 us -> 8.56 us
  local copies, waits for them, and re-layouts: 23 us -> 17 us
    pallas_call x12 -> x2, Pallas kernels: 27.7 us -> 102 us  [the longest x1 90.6 us: reduce_products(): pl.pallas_call(reduce_kernel, in_specs=[pl.BlockSpec(memory_space=pltpu.V...]
    ppermute x21 -> x1, waiting for transfers between devices: 48.6 us -> 0.01 us  [reduced_patch(): other_bin = lax.ppermute(slant_bin, 'dir', [(0, 1), (1, 0)])]
    ppermute x21 -> x1, starting transfers between devices: 34.2 us -> 2.54 us  [reduced_patch(): other_bin = lax.ppermute(slant_bin, 'dir', [(0, 1), (1, 0)])]
    slice x4 -> x0, local copies, waits for them, and re-layouts: 2.67 us -> none  [reduced_patch(): first_kept, first_moved = (arrived[chunk][:1], arrived[chunk][1:])]
    unnamed x22 -> x20, local copies, waits for them, and re-layouts: 9.53 us -> 7.34 us
    another operation x15 -> x16, other arithmetic: 7.03 us -> 7.04 us
  transfers between devices with their start and end apart: 23 -> 3, of which waited for: 9 -> 1; matrix products, arithmetic and copies ran while one was open for 4% -> 3% of each run, Pallas kernels for 14% -> 3%
where the time goes in v1:
time: 211 us; the launch traced here: 210 us
  Pallas kernels  130 us (62%)
  waiting for transfers between devices  20.8 us (10%)
  local copies, waits for them, and re-layouts  17 us (8%)
  blocking collectives  13.3 us (6%)
  other arithmetic  12 us (6%)
  starting transfers between devices  8.56 us (4%)
  matrix products  5.08 us (2%)
  between operations  3.03 us (1%)
    pallas_call x1, Pallas kernels, reduce_products(): pl.pallas_call(reduce_kernel, in_specs=[pl.BlockSpec(memory_space=pltpu.V...  90.6 us
    pallas_call x1, Pallas kernels, half_screens(): pl.pallas_call(screen_kernel, grid=(rows_here // step,), in_specs=[pl.Blo...  21.5 us
    all_to_all x1, waiting for transfers between devices, body(): lax.all_to_all(stacked_field, 'row', split_axis=1, concat_axis=3, tiled=T...  20.8 us
    all_to_all x1, blocking collectives, body(): lax.all_to_all(terms.transpose(1, 0, 2), ('dir', 'row'), split_axis=0, co...  13.3 us
    pallas_call x1, Pallas kernels, patch_products(): pl.pallas_call(product_kernel, grid=(chunks, sides), in_specs=[pl.BlockSp...  11.6 us
    unnamed x20, local copies, waits for them, and re-layouts  7.34 us
    another operation x15, other arithmetic  6.96 us
    pallas_call x1, Pallas kernels, patch_matrix(): pl.pallas_call(matrix_kernel, grid=(length // SECOND,), in_specs=[pl.Bloc...  6.24 us
  transfers between devices with their start and end apart: 3, of which 1 were waited for; matrix products, arithmetic and copies ran while one was open for 3% of the time, Pallas kernels for 3%

profile of v1, /device:TPU:0, one launch (start us, length us, event | category | flops | bytes accessed | tf_op | source)
XLA Modules:
  0.0 209.6 jit_solution(1104559894777889380)
XLA Ops:
  1.0 1.6 copy-done.1
  2.6 1.0 copy-done.2
  3.7 0.9 copy-done.3
  4.6 21.5 %shard_map.113 = (bf16[2,4,2,256,512]{4,3,2,1,0:T(8,128)(2,1)}, bf16[2,4,2,256,512]{4,3,2,1,0:T(8,128)(2,1)}) custom-call(s32[2]{0:T(128)S(1)} %pad_add_fusion.spot, bf16[2,256,8192]{2,1,0:T(8,128)(2,1)} %noise.1, f32[256,1]{1,0:T(8,128)S(1)} %fusion.21.rows_squared, f32[1,8192]{1,0:T(1,128)S(1)} %fusion.55.columns_squared, bf16[256,256]{1,0:T(8,128)(2,1)S(1)} %copy-done.3, ...), custom_call_target="tpu_custom_call" | custom-call | flops 20000000000 | bytes 20000000 | tf_op jit(solution)/shard_map/pallas_call | solution.py:282
  26.4 0.6 fusion.134
  27.0 2.5 %collective-permute-start = (s32[]{:T(128)}, s32[]{:T(128)}, u32[]{:S(2)}, u32[]{:S(2)}) collective-permute-start(s32[]{:T(128)} %bitcast.24), channel_id=1, source_target_pairs={{0,16},{16,0},{1,17},{17,1},{2,18},{18,2},{3,19},{19,3},{4,20},{20... | collective-permute-start | bytes 20 | tf_op jit(solution)/shard_map/ppermute | solution.py:523
  31.8 1.3 add_multiply_fusion.1
  33.4 1.4 copy.127.slow
  34.8 6.2 %shard_map.114.matrix = bf16[1024,1024]{1,0:T(8,128)(2,1)} custom-call(f32[2,1024,4]{2,1,0:T(8,128)} %copy.127.slow, f32[2,128,128]{2,1,0:T(8,128)} %constant.305.clone.fast), custom_call_target="tpu_custom_call" | custom-call | flops 8000000 | bytes 4000000 | tf_op jit(solution)/shard_map/pallas_call | solution.py:332
  41.0 1.6 copy-done
  42.6 2.2 %copy-done.4 = bf16[2,4,2,256,512]{4,3,2,1,0:T(8,128)(2,1)S(1)} copy-done((bf16[2,4,2,256,512]{4,3,2,1,0:T(8,128)(2,1)S(1)}, bf16[2,4,2,256,512]{4,3,2,1,0:T(8,128)(2,1)}, u32[]{:S(2)}) %copy-start.4) | copy-done | bytes 4194328
  44.8 11.6 %shard_map.115.products = bf16[4,2,2,512,512]{4,3,2,1,0:T(8,128)(2,1)S(1)} custom-call(bf16[1024,1024]{1,0:T(8,128)(2,1)S(1)} %copy-done, bf16[2,4,2,256,512]{4,3,2,1,0:T(8,128)(2,1)S(1)} %copy-done.4, bf16[2,4,2,256,512]{4,3,2,1,0:T(8,128)(2,1)} %collective-permute-done.1.received), custom_call_target="tpu_custom_call" | custom-call | flops 8999999488 | bytes 20000000 | tf_op jit(solution)/shard_map/pallas_call | solution.py:369
  56.4 90.6 %shard_map.116 = f32[512,512]{1,0:T(8,128)S(1)} custom-call(bf16[4,2,2,512,512]{4,3,2,1,0:T(8,128)(2,1)S(1)} %shard_map.115.products), custom_call_target="tpu_custom_call" | custom-call | tf_op jit(solution)/shard_map/pallas_call | solution.py:493
  147.0 3.9 %cosine_convert_fusion = (bf16[512,512]{1,0:T(8,128)(2,1)S(1)}, bf16[512,512]{1,0:T(8,128)(2,1)S(1)}) fusion(f32[512,512]{1,0:T(8,128)S(1)} %shard_map.116, f32[]{:T(128)S(6)} %add.505), kind=kLoop, calls=%fused_computation.53 | loop fusion | flops 786432 | bytes 2097156 | tf_op jit(solution)/shard_map/convert.15
  151.6 0.5 convolution_bitcast_fusion.5
  152.5 1.4 convolution_bitcast_fusion.4
  154.3 0.5 convolution_bitcast_fusion.3
  154.7 1.2 copy.208
  156.3 0.5 fusion.1
  156.8 1.6 copy.139
  158.4 5.6 %all-to-all-start = ((bf16[2,16,32,512]{3,2,0,1:T(8,128)(2,1)}), bf16[2,16,32,512]{3,2,0,1:T(8,128)(2,1)S(1)}, u32[]{:S(2)}, u32[]{:S(2)}) async-start(bf16[2,16,32,512]{3,2,0,1:T(8,128)(2,1)} %copy.139), calls=%async_computation | async-start | bytes 2097152 | tf_op jit(solution)/shard_map/all_to_all | solution.py:550
  166.1 20.8 %all-to-all-done = bf16[2,16,32,512]{3,2,0,1:T(8,128)(2,1)S(1)} async-done(((bf16[2,16,32,512]{3,2,0,1:T(8,128)(2,1)}), bf16[2,16,32,512]{3,2,0,1:T(8,128)(2,1)S(1)}, u32[]{:S(2)}, u32[]{:S(2)}) %all-to-all-start) | async-done | bytes 1048608 | tf_op jit(solution)/shard_map/all_to_all | solution.py:550
  187.0 0.6 copy.140
  187.5 0.7 reshape.988
  188.2 0.5 convolution_bitcast_fusion.2
  189.0 0.4 convolution_bitcast_fusion.1
  189.8 0.5 convolution_bitcast_fusion
  190.5 0.5 fusion
  191.6 1.1 fusion.133
  193.2 2.3 %gather_fusion = f32[512]{0:T(512)S(1)} fusion(f32[1024]{0:T(1024)S(1)} %multiply_bitcast_fusion, s32[1024]{0:T(1024)S(1)} %pad_clamp_fusion), kind=kCustom, calls=%fused_computation | custom fusion | bytes 6144 | tf_op jit(solution)/shard_map/jit(_take)/gather | solution.py:567
  195.8 13.3 %all_to_all.20 = f32[32,2,16]{2,1,0:T(2,128)S(1)} all-to-all(f32[32,2,16]{2,1,0:T(2,128)S(1)} %copy.148), channel_id=1, replica_groups=mesh['dir'=2,'row'=16] {'dir','row'}, dimensions={0} | all-to-all | bytes 8192 | tf_op jit(solution)/shard_map/all_to_all | solution.py:575
  209.1 0.5 multiply_bitcast_fusion.1
  (74 shorter events, 7.2 us)
Async XLA Ops:
  1.0 1.6 copy-start.1
  2.6 1.0 copy-start.2
  3.7 0.9 copy-start.3
  4.6 21.9 %copy-start.9 = (s32[1,2]{1,0:T(1,128)S(1)}, s32[1,2]{1,0:T(1,128)}, u32[]{:S(2)}) copy-start(s32[1,2]{1,0:T(1,128)} %param.11) | copy-start | bytes 28
  26.0 15.0 %collective-permute-start.1 = (bf16[2,4,2,256,512]{4,3,2,1,0:T(8,128)(2,1)}, bf16[2,4,2,256,512]{4,3,2,1,0:T(8,128)(2,1)}, u32[]{:S(2)}, u32[]{:S(2)}) collective-permute-start(bf16[2,4,2,256,512]{4,3,2,1,0:T(8,128)(2,1)} %get-tuple-element.9), channel_id=1, source_target_pairs={{0,1},{1,0},{2,3},{3,2},{4,5},{5,4},{6,7},{7,6},{8,9},{9,8},{10,11... | collective-permute-start | bytes 12582920 | tf_op jit(solution)/shard_map/ppermute | solution.py:521
  27.0 4.7 %collective-permute-start = (s32[]{:T(128)}, s32[]{:T(128)}, u32[]{:S(2)}, u32[]{:S(2)}) collective-permute-start(s32[]{:T(128)} %bitcast.24), channel_id=1, source_target_pairs={{0,16},{16,0},{1,17},{17,1},{2,18},{18,2},{3,19},{19,3},{4,20},{20... | collective-permute-start | bytes 20 | tf_op jit(solution)/shard_map/ppermute | solution.py:523
  41.0 1.6 copy-start
  42.6 2.2 %copy-start.4 = (bf16[2,4,2,256,512]{4,3,2,1,0:T(8,128)(2,1)S(1)}, bf16[2,4,2,256,512]{4,3,2,1,0:T(8,128)(2,1)}, u32[]{:S(2)}) copy-start(bf16[2,4,2,256,512]{4,3,2,1,0:T(8,128)(2,1)} %get-tuple-element.8.kept) | copy-start | bytes 12582916
  156.8 7.9 %copy-start.5 = (s32[1,512]{1,0:T(1,128)S(1)}, s32[1,512]{1,0:T(1,128)}, u32[]{:S(2)}) copy-start(s32[1,512]{1,0:T(1,128)} %param.13) | copy-start | bytes 6148
  158.4 28.6 %all-to-all-start = ((bf16[2,16,32,512]{3,2,0,1:T(8,128)(2,1)}), bf16[2,16,32,512]{3,2,0,1:T(8,128)(2,1)S(1)}, u32[]{:S(2)}, u32[]{:S(2)}) async-start(bf16[2,16,32,512]{3,2,0,1:T(8,128)(2,1)} %copy.139), calls=%async_computation | async-start | bytes 2097152 | tf_op jit(solution)/shard_map/all_to_all | solution.py:550
  191.6 3.9 %copy-start.7 = (f32[1,512]{1,0:T(1,128)S(1)}, f32[1,512]{1,0:T(1,128)}, u32[]{:S(2)}) copy-start(f32[1,512]{1,0:T(1,128)} %param.14) | copy-start | bytes 6148
  191.6 3.9 %copy-start.8 = (s32[512]{0:T(512)S(1)}, s32[512]{0:T(512)}, u32[]{:S(2)}) copy-start(s32[512]{0:T(512)} %param.15) | copy-start | bytes 6148
  193.2 16.4 %copy-start.6 = (f32[8,128]{1,0:T(8,128)}, f32[8,128]{1,0:T(8,128)S(1)}, u32[]{:S(2)}) copy-start(f32[8,128]{1,0:T(8,128)S(1)} %fusion.2) | copy-start | bytes 12292

commit v2 on v1

--- a/solution.py
+++ b/solution.py
@@ -518,15 +518,120 @@
     over_core = [(r, r ^ 1) for r in range(row_count)]
     host = host_tables()
     kept, moved = half_screens(white_noise, row_start, row, host)
+    other_bin = lax.ppermute(geometry[0, 1], "dir", [(0, 1), (1, 0)])
+    other_bin, moved = lax.optimization_barrier((other_bin, moved))
     received = lax.ppermute(moved, "row", over_core)
-    slant_bin, kept = lax.optimization_barrier((geometry[0, 1], kept))
-    other_bin = lax.ppermute(slant_bin, "dir", [(0, 1), (1, 0)])
     first_block = 2 * (lax.axis_index("dir") * row_count + row)
     other_block = 2 * (lax.axis_index("dir") * row_count + (row ^ 1))
     block_ids = jnp.stack([first_block, first_block + 1, other_block, other_block + 1])
-    slant_bins = jnp.stack([slant_bin, other_bin])
+    slant_bins = jnp.stack([geometry[0, 1], other_bin])
     matrix = patch_matrix(slant_bins, block_ids, patch_len // SECOND, host[3])
     return reduce_products(patch_products(matrix, kept, received))
+
+
+def turn_kernel(field, result, landed, local_sem, sems):
+    here_dir, row = (lax.axis_index("dir"), lax.axis_index("row"))
+    count = lax.axis_size("row")
+    height = result.shape[1]
+    columns = field.shape[2]
+    mates = [(here_dir, (row + shift) % count) for shift in range(1, count)]
+    barrier = pltpu.get_barrier_semaphore()
+    for mate in mates:
+        pl.semaphore_signal(barrier, inc=1, device_id=mate, device_id_type=pl.DeviceIdType.MESH)
+    pl.semaphore_wait(barrier, len(mates))
+    mine = pl.ds(pl.multiple_of(row * columns, columns), columns)
+
+    def rows_of(spot):
+        return pl.ds(pl.multiple_of(spot * height, height), height)
+
+    copies = [
+        pltpu.make_async_remote_copy(
+            src_ref=field.at[:, rows_of(mate[1]), :],
+            dst_ref=landed.at[:, :, mine],
+            send_sem=sems.at[0, spot],
+            recv_sem=sems.at[1, spot],
+            device_id=mate,
+            device_id_type=pl.DeviceIdType.MESH,
+        )
+        for spot, mate in enumerate(mates)
+    ]
+    for sent in copies:
+        sent.start()
+    local = pltpu.make_async_copy(field.at[:, rows_of(row), :], landed.at[:, :, mine], local_sem)
+    local.start()
+    local.wait()
+    for sent in copies:
+        sent.wait_recv()
+    result[...] = landed[...]
+    for sent in copies:
+        sent.wait_send()
+
+
+def turn_field(field):
+    count = lax.axis_size("row")
+    parts, patch_len, columns = field.shape
+    shape = (parts, patch_len // count, count * columns)
+    return pl.pallas_call(
+        turn_kernel,
+        in_specs=[pl.BlockSpec(memory_space=pltpu.VMEM)],
+        out_specs=pl.BlockSpec(memory_space=pltpu.VMEM),
+        out_shape=jax.ShapeDtypeStruct(shape, field.dtype),
+        scratch_shapes=[
+            pltpu.VMEM(shape, field.dtype),
+            pltpu.SemaphoreType.DMA,
+            pltpu.SemaphoreType.DMA((2, count - 1)),
+        ],
+        compiler_params=pltpu.CompilerParams(
+            collective_id=1, has_side_effects=True, vmem_limit_bytes=16 * 1024 * 1024
+        ),
+    )(field)
+
+
+def share_kernel(terms, result, landed, sems):
+    rows = lax.axis_size("row")
+    count = rows * lax.axis_size("dir")
+    here = lax.axis_index("dir") * rows + lax.axis_index("row")
+    spots = [(here + shift) % count for shift in range(1, count)]
+    mates = [(spot // rows, spot % rows) for spot in spots]
+    barrier = pltpu.get_barrier_semaphore()
+    for mate in mates:
+        pl.semaphore_signal(barrier, inc=1, device_id=mate, device_id_type=pl.DeviceIdType.MESH)
+    pl.semaphore_wait(barrier, len(mates))
+    copies = [
+        pltpu.make_async_remote_copy(
+            src_ref=terms.at[spot],
+            dst_ref=landed.at[place],
+            send_sem=sems.at[0, place],
+            recv_sem=sems.at[1, place],
+            device_id=mate,
+            device_id_type=pl.DeviceIdType.MESH,
+        )
+        for place, (spot, mate) in enumerate(zip(spots, mates))
+    ]
+    for sent in copies:
+        sent.start()
+    total = terms[here]
+    for place, sent in enumerate(copies):
+        sent.wait_recv()
+        total += landed[place]
+    result[...] = total
+    for sent in copies:
+        sent.wait_send()
+
+
+def share_sums(terms):
+    count = terms.shape[0]
+    return pl.pallas_call(
+        share_kernel,
+        in_specs=[pl.BlockSpec(memory_space=pltpu.VMEM)],
+        out_specs=pl.BlockSpec(memory_space=pltpu.VMEM),
+        out_shape=jax.ShapeDtypeStruct(terms.shape[1:], terms.dtype),
+        scratch_shapes=[
+            pltpu.VMEM((count - 1, *terms.shape[1:]), terms.dtype),
+            pltpu.SemaphoreType.DMA((2, count - 1)),
+        ],
+        compiler_params=pltpu.CompilerParams(collective_id=2, has_side_effects=True),
+    )(terms)
 
 
 def body(white_noise, geometry, window, tile_map, link_gain, serving):
@@ -539,15 +644,19 @@
     slant_factor = 1.0 + 0.25 * geometry[0, 1].astype(jnp.float32)
     fresnel_x = fresnel_factor(geometry[0], FIRST, SECOND)
     fresnel_y = fresnel_factor(geometry[0], row_count, ROWS_DEV)
-    if lax.axis_size("dir") == 2 and row_count == 16 and rows_here == 2 * SECOND:
+    direct = lax.axis_size("dir") == 2 and row_count == 16 and rows_here == 2 * SECOND
+    if direct:
         phase_patch = reduced_patch(white_noise, row_start, geometry)
     else:
         half_screen = half_screen_rows(white_noise, row_start, tables)
         phase_patch = gathered_patch(half_screen, geometry, tables, patch_len)
     columns = phase_patch.shape[1]
     screen_field = propagate_columns(phase_patch, tables_y, slant_factor, fresnel_y)
-    stacked_field = screen_field.reshape(2, row_count, ROWS_DEV, columns)
-    portion = lax.all_to_all(stacked_field, "row", split_axis=1, concat_axis=3, tiled=True)
+    if direct:
+        portion = turn_field(screen_field)[:, None]
+    else:
+        stacked_field = screen_field.reshape(2, row_count, ROWS_DEV, columns)
+        portion = lax.all_to_all(stacked_field, "row", split_axis=1, concat_axis=3, tiled=True)
     item_count = portion.shape[2]
     stacked = portion.reshape(2, item_count, FIRST, SECOND)
     spectral = forward_axis(stacked, tables, fresnel_x, row_patterns, False)
@@ -572,10 +681,19 @@
     interference_part = jnp.where(serves_here, 0.0, received)
     device_count = lax.axis_size(("dir", "row"))
     terms = jnp.stack([signal_part, interference_part]).reshape(2, device_count, -1)
-    gathered = lax.all_to_all(
-        terms.transpose(1, 0, 2), ("dir", "row"), split_axis=0, concat_axis=0, tiled=True
-    )
-    signal, interference = jnp.sum(gathered, axis=0)
+    if direct:
+        share = terms.shape[2]
+        padded = jnp.pad(
+            terms.transpose(1, 0, 2).reshape(device_count, 1, 2 * share),
+            ((0, 0), (0, 0), (0, SECOND - 2 * share)),
+        )
+        summed = share_sums(padded)[0]
+        signal, interference = (summed[:share], summed[share : 2 * share])
+    else:
+        gathered = lax.all_to_all(
+            terms.transpose(1, 0, 2), ("dir", "row"), split_axis=0, concat_axis=0, tiled=True
+        )
+        signal, interference = jnp.sum(gathered, axis=0)
     signal_ratio = jnp.log10(signal / (interference + noise_floor))
     return (fluctuation[None], signal_ratio)
 

time: 211 us -> 207 us (0.981)
  Pallas kernels: 130 us -> 166 us
  waiting for transfers between devices: 20.8 us -> 0.01 us
  blocking collectives: 13.3 us -> 0 us
  starting transfers between devices: 8.56 us -> 2.94 us
    pallas_call x0 -> x2, Pallas kernels: none -> 35.9 us  [the longest x1 21.5 us: turn_field(): pl.pallas_call(turn_kernel, in_specs=[pl.BlockSpec(memory_space=pltpu.VME...]
    all_to_all x1 -> x0, waiting for transfers between devices: 20.8 us -> none  [body(): lax.all_to_all(stacked_field, 'row', split_axis=1, concat_axis=3, tiled=T...]
    all_to_all x1 -> x0, blocking collectives: 13.3 us -> none  [body(): lax.all_to_all(terms.transpose(1, 0, 2), ('dir', 'row'), split_axis=0, co...]
    all_to_all x1 -> x0, starting transfers between devices: 5.63 us -> none  [body(): lax.all_to_all(stacked_field, 'row', split_axis=1, concat_axis=3, tiled=T...]
    unnamed x20 -> x19, local copies, waits for them, and re-layouts: 7.34 us -> 7.6 us
  transfers between devices with their start and end apart: 3 -> 2, of which waited for: 1 -> 0; matrix products, arithmetic and copies ran while one was open for 3% -> 3% of each run, Pallas kernels for 3% -> 13%
where the time goes in v2:
time: 207 us; the launch traced here: 206 us
  Pallas kernels  166 us (80%)
  local copies, waits for them, and re-layouts  16.4 us (8%)
  other arithmetic  12.6 us (6%)
  matrix products  5.02 us (2%)
  between operations  2.96 us (1%)
  starting transfers between devices  2.94 us (1%)
    pallas_call x1, Pallas kernels, reduce_products(): pl.pallas_call(reduce_kernel, in_specs=[pl.BlockSpec(memory_space=pltpu.V...  91.3 us
    pallas_call x1, Pallas kernels, turn_field(): pl.pallas_call(turn_kernel, in_specs=[pl.BlockSpec(memory_space=pltpu.VME...  21.5 us
    pallas_call x1, Pallas kernels, half_screens(): pl.pallas_call(screen_kernel, grid=(rows_here // step,), in_specs=[pl.Blo...  21.4 us
    pallas_call x1, Pallas kernels, share_sums(): pl.pallas_call(share_kernel, in_specs=[pl.BlockSpec(memory_space=pltpu.VM...  14.4 us
    pallas_call x1, Pallas kernels, patch_products(): pl.pallas_call(product_kernel, grid=(chunks, sides), in_specs=[pl.BlockSp...  11.6 us
    unnamed x19, local copies, waits for them, and re-layouts  7.6 us
    another operation x15, other arithmetic  6.95 us
    pallas_call x1, Pallas kernels, patch_matrix(): pl.pallas_call(matrix_kernel, grid=(length // SECOND,), in_specs=[pl.Bloc...  6.24 us
  transfers between devices with their start and end apart: 2, of which 0 were waited for; matrix products, arithmetic and copies ran while one was open for 3% of the time, Pallas kernels for 13%

profile of v2, /device:TPU:0, one launch (start us, length us, event | category | flops | bytes accessed | tf_op | source)
XLA Modules:
  0.0 206.4 jit_solution(13208916458179839830)
XLA Ops:
  0.6 1.3 fusion.136
  1.9 2.9 %collective-permute-start = (s32[]{:T(128)}, s32[]{:T(128)}, u32[]{:S(2)}, u32[]{:S(2)}) collective-permute-start(s32[]{:T(128)} %bitcast.24), channel_id=1, source_target_pairs={{0,16},{16,0},{1,17},{17,1},{2,18},{18,2},{3,19},{19,3},{4,20},{20... | collective-permute-start | bytes 20 | tf_op jit(solution)/shard_map/ppermute | solution.py:521
  5.3 1.6 copy-done.1
  6.8 1.0 copy-done.2
  7.9 0.9 copy-done.3
  8.8 21.4 %shard_map.113 = (bf16[2,4,2,256,512]{4,3,2,1,0:T(8,128)(2,1)}, bf16[2,4,2,256,512]{4,3,2,1,0:T(8,128)(2,1)}) custom-call(s32[2]{0:T(128)S(1)} %pad_add_fusion.spot, bf16[2,256,8192]{2,1,0:T(8,128)(2,1)} %noise.1, f32[256,1]{1,0:T(8,128)S(1)} %fusion.23.rows_squared, f32[1,8192]{1,0:T(1,128)S(1)} %fusion.57.columns_squared, bf16[256,256]{1,0:T(8,128)(2,1)S(1)} %copy-done.3, ...), custom_call_target="tpu_custom_call" | custom-call | flops 20000000000 | bytes 20000000 | tf_op jit(solution)/shard_map/pallas_call | solution.py:282
  34.5 1.3 add_multiply_fusion.1
  36.1 1.4 copy.134.slow
  37.5 6.2 %shard_map.114.matrix = bf16[1024,1024]{1,0:T(8,128)(2,1)} custom-call(f32[2,1024,4]{2,1,0:T(8,128)} %copy.134.slow, f32[2,128,128]{2,1,0:T(8,128)} %constant.306.clone.fast), custom_call_target="tpu_custom_call" | custom-call | flops 8000000 | bytes 4000000 | tf_op jit(solution)/shard_map/pallas_call | solution.py:332
  43.8 1.6 copy-done
  45.3 2.2 %copy-done.4 = bf16[2,4,2,256,512]{4,3,2,1,0:T(8,128)(2,1)S(1)} copy-done((bf16[2,4,2,256,512]{4,3,2,1,0:T(8,128)(2,1)S(1)}, bf16[2,4,2,256,512]{4,3,2,1,0:T(8,128)(2,1)}, u32[]{:S(2)}) %copy-start.4) | copy-done | bytes 4194328
  47.5 11.6 %shard_map.115.products = bf16[4,2,2,512,512]{4,3,2,1,0:T(8,128)(2,1)S(1)} custom-call(bf16[1024,1024]{1,0:T(8,128)(2,1)S(1)} %copy-done, bf16[2,4,2,256,512]{4,3,2,1,0:T(8,128)(2,1)S(1)} %copy-done.4, bf16[2,4,2,256,512]{4,3,2,1,0:T(8,128)(2,1)} %collective-permute-done.1.received), custom_call_target="tpu_custom_call" | custom-call | flops 8999999488 | bytes 20000000 | tf_op jit(solution)/shard_map/pallas_call | solution.py:369
  59.1 91.3 %shard_map.116 = f32[512,512]{1,0:T(8,128)S(1)} custom-call(bf16[4,2,2,512,512]{4,3,2,1,0:T(8,128)(2,1)S(1)} %shard_map.115.products), custom_call_target="tpu_custom_call" | custom-call | tf_op jit(solution)/shard_map/pallas_call | solution.py:493
  150.4 3.9 %cosine_convert_fusion = (bf16[512,512]{1,0:T(8,128)(2,1)S(1)}, bf16[512,512]{1,0:T(8,128)(2,1)S(1)}) fusion(f32[512,512]{1,0:T(8,128)S(1)} %shard_map.116, f32[]{:T(128)S(6)} %add.507), kind=kLoop, calls=%fused_computation.55 | loop fusion | flops 786432 | bytes 2097156 | tf_op jit(solution)/shard_map/convert.15
  154.9 0.5 convolution_bitcast_fusion.5
  155.8 1.4 convolution_bitcast_fusion.4
  157.3 0.3 subtract_convert_fusion.4
  157.6 0.5 convolution_bitcast_fusion.3
  158.1 1.2 copy.221
  159.6 0.5 fusion.1
  160.1 0.6 copy.146
  160.7 21.5 %shard_map.117 = bf16[2,32,8192]{2,1,0:T(8,128)(2,1)S(1)} custom-call(bf16[2,512,512]{2,1,0:T(8,128)(2,1)S(1)} %bitcast.172), custom_call_target="tpu_custom_call" | custom-call | tf_op jit(solution)/shard_map/pallas_call | solution.py:574
  182.5 0.5 convolution_bitcast_fusion.2
  183.3 0.4 convolution_bitcast_fusion.1
  184.0 0.5 convolution_bitcast_fusion
  184.8 0.5 fusion
  185.4 0.3 add.541
  185.8 1.1 fusion.135
  187.4 2.3 %gather_fusion = f32[512]{0:T(512)S(1)} fusion(f32[1024]{0:T(1024)S(1)} %multiply_bitcast_fusion, s32[1024]{0:T(1024)S(1)} %pad_clamp_fusion), kind=kCustom, calls=%fused_computation | custom fusion | bytes 6144 | tf_op jit(solution)/shard_map/jit(_take)/gather | solution.py:676
  190.0 0.6 pad.4.terms
  190.7 14.4 %shard_map.118 = f32[1,128]{1,0:T(1,128)} custom-call(f32[32,1,128]{2,1,0:T(1,128)} %pad.4.terms), custom_call_target="tpu_custom_call" | custom-call | tf_op jit(solution)/shard_map/pallas_call | solution.py:624
  205.1 1.3 multiply_bitcast_fusion.1
  (71 shorter events, 6.4 us)
Async XLA Ops:
  1.9 28.2 %collective-permute-start = (s32[]{:T(128)}, s32[]{:T(128)}, u32[]{:S(2)}, u32[]{:S(2)}) collective-permute-start(s32[]{:T(128)} %bitcast.24), channel_id=1, source_target_pairs={{0,16},{16,0},{1,17},{17,1},{2,18},{18,2},{3,19},{19,3},{4,20},{20... | collective-permute-start | bytes 20 | tf_op jit(solution)/shard_map/ppermute | solution.py:521
  5.2 1.6 copy-start.1
  6.8 1.0 copy-start.2
  7.9 0.9 copy-start.3
  8.8 23.9 %copy-start.5 = (s32[1,512]{1,0:T(1,128)S(1)}, s32[1,512]{1,0:T(1,128)}, u32[]{:S(2)}) copy-start(s32[1,512]{1,0:T(1,128)} %param.13) | copy-start | bytes 6148
  30.2 13.6 %collective-permute-start.1 = (bf16[2,4,2,256,512]{4,3,2,1,0:T(8,128)(2,1)}, bf16[2,4,2,256,512]{4,3,2,1,0:T(8,128)(2,1)}, u32[]{:S(2)}, u32[]{:S(2)}) collective-permute-start(bf16[2,4,2,256,512]{4,3,2,1,0:T(8,128)(2,1)} %get-tuple-element.9), channel_id=1, source_target_pairs={{0,1},{1,0},{2,3},{3,2},{4,5},{5,4},{6,7},{7,6},{8,9},{9,8},{10,11... | collective-permute-start | bytes 12582920 | tf_op jit(solution)/shard_map/ppermute | solution.py:523
  43.8 1.6 copy-start
  45.3 2.2 %copy-start.4 = (bf16[2,4,2,256,512]{4,3,2,1,0:T(8,128)(2,1)S(1)}, bf16[2,4,2,256,512]{4,3,2,1,0:T(8,128)(2,1)}, u32[]{:S(2)}) copy-start(bf16[2,4,2,256,512]{4,3,2,1,0:T(8,128)(2,1)} %get-tuple-element.8.kept) | copy-start | bytes 12582916
  185.8 3.9 %copy-start.7 = (f32[1,512]{1,0:T(1,128)S(1)}, f32[1,512]{1,0:T(1,128)}, u32[]{:S(2)}) copy-start(f32[1,512]{1,0:T(1,128)} %param.14) | copy-start | bytes 6148
  185.8 3.9 %copy-start.8 = (s32[512]{0:T(512)S(1)}, s32[512]{0:T(512)}, u32[]{:S(2)}) copy-start(s32[512]{0:T(512)} %param.15) | copy-start | bytes 6148
  187.3 19.0 %copy-start.6 = (f32[8,128]{1,0:T(8,128)}, f32[8,128]{1,0:T(8,128)S(1)}, u32[]{:S(2)}) copy-start(f32[8,128]{1,0:T(8,128)S(1)} %fusion.2) | copy-start | bytes 12292

commit v3 on v2

--- a/solution.py
+++ b/solution.py
@@ -310,16 +310,18 @@
 
 
 def matrix_kernel(slow, fast, matrix):
-    for source in range(2):
-        for near in range(2):
-            block = source * 2 + near
-            slow_real = slow[0, :, block : block + 1]
-            slow_imag = slow[1, :, block : block + 1]
-            real_part = slow_real * fast[0] - slow_imag * fast[1]
-            imag_part = slow_real * fast[1] + slow_imag * fast[0]
-            for z, part in enumerate((real_part, -imag_part)):
-                start = ((source * 2 + z) * 2 + near) * SECOND
-                matrix[:, start : start + SECOND] = part.astype(jnp.bfloat16)
+    for outer in range(matrix.shape[0] // SECOND):
+        rows = slice(outer * SECOND, (outer + 1) * SECOND)
+        for source in range(2):
+            for near in range(2):
+                block = source * 2 + near
+                slow_real = slow[0, rows, block : block + 1]
+                slow_imag = slow[1, rows, block : block + 1]
+                real_part = slow_real * fast[0] - slow_imag * fast[1]
+                imag_part = slow_real * fast[1] + slow_imag * fast[0]
+                for z, part in enumerate((real_part, -imag_part)):
+                    start = ((source * 2 + z) * 2 + near) * SECOND
+                    matrix[rows, start : start + SECOND] = part.astype(jnp.bfloat16)
 
 
 def patch_matrix(slant_bins, block_ids, outer_count, fast):
@@ -331,12 +333,12 @@
     length = position.shape[0]
     return pl.pallas_call(
         matrix_kernel,
-        grid=(length // SECOND,),
+        grid=(2,),
         in_specs=[
-            pl.BlockSpec((2, SECOND, 4), lambda i: (0, i, 0)),
+            pl.BlockSpec((2, length // 2, 4), lambda i: (0, i, 0)),
             pl.BlockSpec(fast.shape, lambda i: (0, 0, 0)),
         ],
-        out_specs=pl.BlockSpec((SECOND, 8 * SECOND), lambda i: (i, 0)),
+        out_specs=pl.BlockSpec((length // 2, 8 * SECOND), lambda i: (i, 0)),
         out_shape=jax.ShapeDtypeStruct((length, 8 * SECOND), jnp.bfloat16),
         cost_estimate=pl.CostEstimate(
             flops=8_000_000, bytes_accessed=4_000_000, transcendentals=0
@@ -456,10 +458,12 @@
             sent.start()
 
     count = len(units)
-    ahead = 4
+    ahead = 2
     for unit in range(ahead):
         a_copies[unit].start()
     for unit, (chunk, _) in enumerate(units):
+        if unit >= 2:
+            finish(unit - 2)
         a_copies[unit].wait_recv()
         side = (0, 1) if chunk % 2 == 0 else (1, 0)
         b_send[unit] = (
@@ -469,8 +473,6 @@
         b_copies[unit].start()
         if unit + ahead < count:
             a_copies[unit + ahead].start()
-        if unit >= 2:
-            finish(unit - 2)
     finish(count - 2)
     finish(count - 1)
     for unit, (chunk, _) in enumerate(units):
@@ -518,13 +520,13 @@
     over_core = [(r, r ^ 1) for r in range(row_count)]
     host = host_tables()
     kept, moved = half_screens(white_noise, row_start, row, host)
-    other_bin = lax.ppermute(geometry[0, 1], "dir", [(0, 1), (1, 0)])
-    other_bin, moved = lax.optimization_barrier((other_bin, moved))
     received = lax.ppermute(moved, "row", over_core)
+    slant_bin, kept = lax.optimization_barrier((geometry[0, 1], kept))
+    other_bin = lax.ppermute(slant_bin, "dir", [(0, 1), (1, 0)])
     first_block = 2 * (lax.axis_index("dir") * row_count + row)
     other_block = 2 * (lax.axis_index("dir") * row_count + (row ^ 1))
     block_ids = jnp.stack([first_block, first_block + 1, other_block, other_block + 1])
-    slant_bins = jnp.stack([geometry[0, 1], other_bin])
+    slant_bins = jnp.stack([slant_bin, other_bin])
     matrix = patch_matrix(slant_bins, block_ids, patch_len // SECOND, host[3])
     return reduce_products(patch_products(matrix, kept, received))
 

time: 207 us -> 199 us (0.961)
  Pallas kernels: 166 us -> 159 us
    pallas_call x1, Pallas kernels: 91.3 us -> 85.9 us  [reduce_products(): pl.pallas_call(reduce_kernel, in_specs=[pl.BlockSpec(memory_space=pltpu.V...]
    pallas_call x1, Pallas kernels: 6.24 us -> 3.34 us  [patch_matrix(): pl.pallas_call(matrix_kernel, grid=(2,), in_specs=[pl.BlockSpec((2, lengt...]
    unnamed x19 -> x21, local copies, waits for them, and re-layouts: 7.6 us -> 7.61 us
  transfers between devices with their start and end apart: 2 -> 2, of which waited for: 0 -> 0; matrix products, arithmetic and copies ran while one was open for 3% -> 3% of each run, Pallas kernels for 13% -> 2%
where the time goes in v3:
time: 199 us; the launch traced here: 198 us
  Pallas kernels  159 us (80%)
  local copies, waits for them, and re-layouts  15.7 us (8%)
  other arithmetic  12.7 us (6%)
  matrix products  5.03 us (3%)
  between operations  3.03 us (2%)
  starting transfers between devices  2.95 us (1%)
    pallas_call x1, Pallas kernels, reduce_products(): pl.pallas_call(reduce_kernel, in_specs=[pl.BlockSpec(memory_space=pltpu.V...  85.9 us
    pallas_call x1, Pallas kernels, turn_field(): pl.pallas_call(turn_kernel, in_specs=[pl.BlockSpec(memory_space=pltpu.VME...  22 us
    pallas_call x1, Pallas kernels, half_screens(): pl.pallas_call(screen_kernel, grid=(rows_here // step,), in_specs=[pl.Blo...  21.4 us
    pallas_call x1, Pallas kernels, share_sums(): pl.pallas_call(share_kernel, in_specs=[pl.BlockSpec(memory_space=pltpu.VM...  14.4 us
    pallas_call x1, Pallas kernels, patch_products(): pl.pallas_call(product_kernel, grid=(chunks, sides), in_specs=[pl.BlockSp...  11.6 us
    unnamed x21, local copies, waits for them, and re-layouts  7.61 us
    another operation x15, other arithmetic  6.95 us
    dot_general x8, matrix products, contract(): jnp.einsum(pattern, operand, matrix, preferred_element_type=jnp.float32)  4.69 us
  transfers between devices with their start and end apart: 2, of which 0 were waited for; matrix products, arithmetic and copies ran while one was open for 3% of the time, Pallas kernels for 2%

profile of v3, /device:TPU:0, one launch (start us, length us, event | category | flops | bytes accessed | tf_op | source)
XLA Modules:
  0.0 198.0 jit_solution(10459320376101129532)
XLA Ops:
  1.0 1.6 copy-done.1
  2.6 1.0 copy-done.2
  3.7 0.9 copy-done.3
  4.6 21.4 %shard_map.113 = (bf16[2,4,2,256,512]{4,3,2,1,0:T(8,128)(2,1)}, bf16[2,4,2,256,512]{4,3,2,1,0:T(8,128)(2,1)}) custom-call(s32[2]{0:T(128)S(1)} %pad_add_fusion.spot, bf16[2,256,8192]{2,1,0:T(8,128)(2,1)} %noise.1, f32[256,1]{1,0:T(8,128)S(1)} %fusion.23.rows_squared, f32[1,8192]{1,0:T(1,128)S(1)} %fusion.57.columns_squared, bf16[256,256]{1,0:T(8,128)(2,1)S(1)} %copy-done.3, ...), custom_call_target="tpu_custom_call" | custom-call | flops 20000000000 | bytes 20000000 | tf_op jit(solution)/shard_map/pallas_call | solution.py:282
  26.0 0.5 collective-permute-start.1
  26.4 0.6 fusion.136
  27.0 2.5 %collective-permute-start = (s32[]{:T(128)}, s32[]{:T(128)}, u32[]{:S(2)}, u32[]{:S(2)}) collective-permute-start(s32[]{:T(128)} %bitcast.24), channel_id=1, source_target_pairs={{0,16},{16,0},{1,17},{17,1},{2,18},{18,2},{3,19},{19,3},{4,20},{20... | collective-permute-start | bytes 20 | tf_op jit(solution)/shard_map/ppermute | solution.py:525
  33.8 1.3 add_multiply_fusion.1
  35.5 1.4 copy.134.slow
  36.9 3.3 %shard_map.114.matrix = bf16[1024,1024]{1,0:T(8,128)(2,1)} custom-call(f32[2,1024,4]{2,1,0:T(8,128)} %copy.134.slow, f32[2,128,128]{2,1,0:T(8,128)} %constant.306.clone.fast), custom_call_target="tpu_custom_call" | custom-call | flops 8000000 | bytes 4000000 | tf_op jit(solution)/shard_map/pallas_call | solution.py:334
  40.2 1.6 copy-done
  41.8 2.2 %copy-done.4 = bf16[2,4,2,256,512]{4,3,2,1,0:T(8,128)(2,1)S(1)} copy-done((bf16[2,4,2,256,512]{4,3,2,1,0:T(8,128)(2,1)S(1)}, bf16[2,4,2,256,512]{4,3,2,1,0:T(8,128)(2,1)}, u32[]{:S(2)}) %copy-start.4) | copy-done | bytes 4194328
  44.0 11.6 %shard_map.115.products = bf16[4,2,2,512,512]{4,3,2,1,0:T(8,128)(2,1)S(1)} custom-call(bf16[1024,1024]{1,0:T(8,128)(2,1)S(1)} %copy-done, bf16[2,4,2,256,512]{4,3,2,1,0:T(8,128)(2,1)S(1)} %copy-done.4, bf16[2,4,2,256,512]{4,3,2,1,0:T(8,128)(2,1)} %collective-permute-done.1.received), custom_call_target="tpu_custom_call" | custom-call | flops 8999999488 | bytes 20000000 | tf_op jit(solution)/shard_map/pallas_call | solution.py:371
  55.6 85.9 %shard_map.116 = f32[512,512]{1,0:T(8,128)S(1)} custom-call(bf16[4,2,2,512,512]{4,3,2,1,0:T(8,128)(2,1)S(1)} %shard_map.115.products), custom_call_target="tpu_custom_call" | custom-call | tf_op jit(solution)/shard_map/pallas_call | solution.py:495
  141.5 3.9 %cosine_convert_fusion = (bf16[512,512]{1,0:T(8,128)(2,1)S(1)}, bf16[512,512]{1,0:T(8,128)(2,1)S(1)}) fusion(f32[512,512]{1,0:T(8,128)S(1)} %shard_map.116, f32[]{:T(128)S(6)} %add.507), kind=kLoop, calls=%fused_computation.55 | loop fusion | flops 786432 | bytes 2097156 | tf_op jit(solution)/shard_map/convert.15
  146.0 0.5 convolution_bitcast_fusion.5
  146.9 1.4 convolution_bitcast_fusion.4
  148.7 0.5 convolution_bitcast_fusion.3
  149.2 1.2 copy.221
  150.7 0.5 fusion.1
  151.2 0.6 copy.146
  151.8 22.0 %shard_map.117 = bf16[2,32,8192]{2,1,0:T(8,128)(2,1)S(1)} custom-call(bf16[2,512,512]{2,1,0:T(8,128)(2,1)S(1)} %bitcast.172), custom_call_target="tpu_custom_call" | custom-call | tf_op jit(solution)/shard_map/pallas_call | solution.py:576
  174.0 0.5 convolution_bitcast_fusion.2
  174.8 0.4 convolution_bitcast_fusion.1
  175.6 0.5 convolution_bitcast_fusion
  176.4 0.5 fusion
  177.0 0.3 add.541
  177.4 1.1 fusion.135
  178.9 2.3 %gather_fusion = f32[512]{0:T(512)S(1)} fusion(f32[1024]{0:T(1024)S(1)} %multiply_bitcast_fusion, s32[1024]{0:T(1024)S(1)} %pad_clamp_fusion), kind=kCustom, calls=%fused_computation | custom fusion | bytes 6144 | tf_op jit(solution)/shard_map/jit(_take)/gather | solution.py:678
  181.6 0.6 pad.4.terms
  182.2 14.4 %shard_map.118 = f32[1,128]{1,0:T(1,128)} custom-call(f32[32,1,128]{2,1,0:T(1,128)} %pad.4.terms), custom_call_target="tpu_custom_call" | custom-call | tf_op jit(solution)/shard_map/pallas_call | solution.py:626
  196.7 1.3 multiply_bitcast_fusion.1
  (73 shorter events, 6.7 us)
Async XLA Ops:
  1.0 1.6 copy-start.1
  2.6 1.0 copy-start.2
  3.7 0.9 copy-start.3
  4.6 21.9 %copy-start.9 = (s32[1,2]{1,0:T(1,128)S(1)}, s32[1,2]{1,0:T(1,128)}, u32[]{:S(2)}) copy-start(s32[1,2]{1,0:T(1,128)} %param.11) | copy-start | bytes 28
  4.6 27.5 %copy-start.5 = (s32[1,512]{1,0:T(1,128)S(1)}, s32[1,512]{1,0:T(1,128)}, u32[]{:S(2)}) copy-start(s32[1,512]{1,0:T(1,128)} %param.13) | copy-start | bytes 6148
  26.0 14.3 %collective-permute-start.1 = (bf16[2,4,2,256,512]{4,3,2,1,0:T(8,128)(2,1)}, bf16[2,4,2,256,512]{4,3,2,1,0:T(8,128)(2,1)}, u32[]{:S(2)}, u32[]{:S(2)}) collective-permute-start(bf16[2,4,2,256,512]{4,3,2,1,0:T(8,128)(2,1)} %get-tuple-element.9), channel_id=1, source_target_pairs={{0,1},{1,0},{2,3},{3,2},{4,5},{5,4},{6,7},{7,6},{8,9},{9,8},{10,11... | collective-permute-start | bytes 12582920 | tf_op jit(solution)/shard_map/ppermute | solution.py:523
  27.0 6.8 %collective-permute-start = (s32[]{:T(128)}, s32[]{:T(128)}, u32[]{:S(2)}, u32[]{:S(2)}) collective-permute-start(s32[]{:T(128)} %bitcast.24), channel_id=1, source_target_pairs={{0,16},{16,0},{1,17},{17,1},{2,18},{18,2},{3,19},{19,3},{4,20},{20... | collective-permute-start | bytes 20 | tf_op jit(solution)/shard_map/ppermute | solution.py:525
  40.2 1.6 copy-start
  41.8 2.2 %copy-start.4 = (bf16[2,4,2,256,512]{4,3,2,1,0:T(8,128)(2,1)S(1)}, bf16[2,4,2,256,512]{4,3,2,1,0:T(8,128)(2,1)}, u32[]{:S(2)}) copy-start(bf16[2,4,2,256,512]{4,3,2,1,0:T(8,128)(2,1)} %get-tuple-element.8.kept) | copy-start | bytes 12582916
  177.3 3.9 %copy-start.7 = (f32[1,512]{1,0:T(1,128)S(1)}, f32[1,512]{1,0:T(1,128)}, u32[]{:S(2)}) copy-start(f32[1,512]{1,0:T(1,128)} %param.14) | copy-start | bytes 6148
  177.3 3.9 %copy-start.8 = (s32[512]{0:T(512)S(1)}, s32[512]{0:T(512)}, u32[]{:S(2)}) copy-start(s32[512]{0:T(512)} %param.15) | copy-start | bytes 6148
  178.9 19.1 %copy-start.6 = (f32[8,128]{1,0:T(8,128)}, f32[8,128]{1,0:T(8,128)S(1)}, u32[]{:S(2)}) copy-start(f32[8,128]{1,0:T(8,128)S(1)} %fusion.2) | copy-start | bytes 12292

commit v4 on v3

--- a/solution.py
+++ b/solution.py
@@ -589,51 +589,71 @@
     )(field)
 
 
-def share_kernel(terms, result, landed, sems):
-    rows = lax.axis_size("row")
-    count = rows * lax.axis_size("dir")
-    here = lax.axis_index("dir") * rows + lax.axis_index("row")
+def share_kernel(terms, result, landed, planes, landed_planes, sems, plane_sems):
+    here_dir, row = (lax.axis_index("dir"), lax.axis_index("row"))
+    plane, low = (row // 4, row % 4)
+    count, depth = (terms.shape[0], terms.shape[1])
+    here = here_dir * 4 + low
     spots = [(here + shift) % count for shift in range(1, count)]
-    mates = [(spot // rows, spot % rows) for spot in spots]
+    mates = [(spot // 4, plane * 4 + spot % 4) for spot in spots]
+    plane_spots = [(plane + shift) % depth for shift in range(1, depth)]
+    plane_mates = [(here_dir, spot * 4 + low) for spot in plane_spots]
     barrier = pltpu.get_barrier_semaphore()
-    for mate in mates:
+    for mate in mates + plane_mates:
         pl.semaphore_signal(barrier, inc=1, device_id=mate, device_id_type=pl.DeviceIdType.MESH)
-    pl.semaphore_wait(barrier, len(mates))
-    copies = [
-        pltpu.make_async_remote_copy(
-            src_ref=terms.at[spot],
-            dst_ref=landed.at[place],
-            send_sem=sems.at[0, place],
-            recv_sem=sems.at[1, place],
-            device_id=mate,
-            device_id_type=pl.DeviceIdType.MESH,
-        )
-        for place, (spot, mate) in enumerate(zip(spots, mates))
-    ]
-    for sent in copies:
-        sent.start()
+    pl.semaphore_wait(barrier, len(mates) + len(plane_mates))
+
+    def exchange(source, target, semaphores, places, devices):
+        copies = [
+            pltpu.make_async_remote_copy(
+                src_ref=source.at[spot],
+                dst_ref=target.at[place],
+                send_sem=semaphores.at[0, place],
+                recv_sem=semaphores.at[1, place],
+                device_id=mate,
+                device_id_type=pl.DeviceIdType.MESH,
+            )
+            for place, (spot, mate) in enumerate(zip(places, devices))
+        ]
+        for sent in copies:
+            sent.start()
+        return copies
+
+    copies = exchange(terms, landed, sems, spots, mates)
     total = terms[here]
     for place, sent in enumerate(copies):
         sent.wait_recv()
         total += landed[place]
+    planes[...] = total
+    plane_copies = exchange(planes, landed_planes, plane_sems, plane_spots, plane_mates)
+    total = planes[plane]
+    for place, sent in enumerate(plane_copies):
+        sent.wait_recv()
+        total += landed_planes[place]
     result[...] = total
-    for sent in copies:
+    for sent in copies + plane_copies:
         sent.wait_send()
 
 
 def share_sums(terms):
-    count = terms.shape[0]
+    lanes = terms.shape[2]
+    count, depth = (8, terms.shape[0] // 8)
+    ordered = terms.reshape(2, depth, 4, 1, lanes).transpose(0, 2, 1, 3, 4)
+    ordered = ordered.reshape(count, depth, 1, lanes)
     return pl.pallas_call(
         share_kernel,
         in_specs=[pl.BlockSpec(memory_space=pltpu.VMEM)],
         out_specs=pl.BlockSpec(memory_space=pltpu.VMEM),
-        out_shape=jax.ShapeDtypeStruct(terms.shape[1:], terms.dtype),
+        out_shape=jax.ShapeDtypeStruct((1, lanes), terms.dtype),
         scratch_shapes=[
-            pltpu.VMEM((count - 1, *terms.shape[1:]), terms.dtype),
+            pltpu.VMEM((count - 1, depth, 1, lanes), terms.dtype),
+            pltpu.VMEM((depth, 1, lanes), terms.dtype),
+            pltpu.VMEM((depth - 1, 1, lanes), terms.dtype),
             pltpu.SemaphoreType.DMA((2, count - 1)),
+            pltpu.SemaphoreType.DMA((2, depth - 1)),
         ],
         compiler_params=pltpu.CompilerParams(collective_id=2, has_side_effects=True),
-    )(terms)
+    )(ordered)
 
 
 def body(white_noise, geometry, window, tile_map, link_gain, serving):

time: 199 us -> 200 us (level)
    unnamed x21 -> x22, local copies, waits for them, and re-layouts: 7.61 us -> 7.68 us
where the time goes in v4:
time: 200 us
  Pallas kernels  160 us (80%)
  local copies, waits for them, and re-layouts  15.7 us (8%)
  other arithmetic  12.7 us (6%)
  matrix products  5.03 us (3%)
  between operations  3.03 us (2%)
  starting transfers between devices  2.95 us (1%)
    pallas_call x1, Pallas kernels, reduce_products(): pl.pallas_call(reduce_kernel, in_specs=[pl.BlockSpec(memory_space=pltpu.V...  85.9 us
    pallas_call x1, Pallas kernels, turn_field(): pl.pallas_call(turn_kernel, in_specs=[pl.BlockSpec(memory_space=pltpu.VME...  22 us
    pallas_call x1, Pallas kernels, half_screens(): pl.pallas_call(screen_kernel, grid=(rows_here // step,), in_specs=[pl.Blo...  21.4 us
    pallas_call x1, Pallas kernels, share_sums(): pl.pallas_call(share_kernel, in_specs=[pl.BlockSpec(memory_space=pltpu.VM...  16 us
    pallas_call x1, Pallas kernels, patch_products(): pl.pallas_call(product_kernel, grid=(chunks, sides), in_specs=[pl.BlockSp...  11.6 us
    unnamed x22, local copies, waits for them, and re-layouts  7.68 us
    another operation x15, other arithmetic  6.95 us
    dot_general x8, matrix products, contract(): jnp.einsum(pattern, operand, matrix, preferred_element_type=jnp.float32)  4.69 us
  transfers between devices with their start and end apart: 2, of which 0 were waited for; matrix products, arithmetic and copies ran while one was open for 3% of the time, Pallas kernels for 2%

profile of v4, /device:TPU:0, one launch (start us, length us, event | category | flops | bytes accessed | tf_op | source)
XLA Modules:
  0.0 199.5 jit_solution(11444992498773947508)
XLA Ops:
  1.0 1.6 copy-done.1
  2.6 1.0 copy-done.2
  3.7 0.9 copy-done.3
  4.6 21.4 %shard_map.113 = (bf16[2,4,2,256,512]{4,3,2,1,0:T(8,128)(2,1)}, bf16[2,4,2,256,512]{4,3,2,1,0:T(8,128)(2,1)}) custom-call(s32[2]{0:T(128)S(1)} %pad_add_fusion.spot, bf16[2,256,8192]{2,1,0:T(8,128)(2,1)} %noise.1, f32[256,1]{1,0:T(8,128)S(1)} %fusion.23.rows_squared, f32[1,8192]{1,0:T(1,128)S(1)} %fusion.57.columns_squared, bf16[256,256]{1,0:T(8,128)(2,1)S(1)} %copy-done.3, ...), custom_call_target="tpu_custom_call" | custom-call | flops 20000000000 | bytes 20000000 | tf_op jit(solution)/shard_map/pallas_call | solution.py:282
  26.0 0.5 collective-permute-start.1
  26.4 0.6 fusion.136
  27.0 2.5 %collective-permute-start = (s32[]{:T(128)}, s32[]{:T(128)}, u32[]{:S(2)}, u32[]{:S(2)}) collective-permute-start(s32[]{:T(128)} %bitcast.24), channel_id=1, source_target_pairs={{0,16},{16,0},{1,17},{17,1},{2,18},{18,2},{3,19},{19,3},{4,20},{20... | collective-permute-start | bytes 20 | tf_op jit(solution)/shard_map/ppermute | solution.py:525
  33.8 1.3 add_multiply_fusion.1
  35.5 1.4 copy.138.slow
  36.9 3.3 %shard_map.114.matrix = bf16[1024,1024]{1,0:T(8,128)(2,1)} custom-call(f32[2,1024,4]{2,1,0:T(8,128)} %copy.138.slow, f32[2,128,128]{2,1,0:T(8,128)} %constant.306.clone.fast), custom_call_target="tpu_custom_call" | custom-call | flops 8000000 | bytes 4000000 | tf_op jit(solution)/shard_map/pallas_call | solution.py:334
  40.2 1.6 copy-done
  41.8 2.2 %copy-done.4 = bf16[2,4,2,256,512]{4,3,2,1,0:T(8,128)(2,1)S(1)} copy-done((bf16[2,4,2,256,512]{4,3,2,1,0:T(8,128)(2,1)S(1)}, bf16[2,4,2,256,512]{4,3,2,1,0:T(8,128)(2,1)}, u32[]{:S(2)}) %copy-start.4) | copy-done | bytes 4194328
  44.0 11.6 %shard_map.115.products = bf16[4,2,2,512,512]{4,3,2,1,0:T(8,128)(2,1)S(1)} custom-call(bf16[1024,1024]{1,0:T(8,128)(2,1)S(1)} %copy-done, bf16[2,4,2,256,512]{4,3,2,1,0:T(8,128)(2,1)S(1)} %copy-done.4, bf16[2,4,2,256,512]{4,3,2,1,0:T(8,128)(2,1)} %collective-permute-done.1.received), custom_call_target="tpu_custom_call" | custom-call | flops 8999999488 | bytes 20000000 | tf_op jit(solution)/shard_map/pallas_call | solution.py:371
  55.6 85.9 %shard_map.116 = f32[512,512]{1,0:T(8,128)S(1)} custom-call(bf16[4,2,2,512,512]{4,3,2,1,0:T(8,128)(2,1)S(1)} %shard_map.115.products), custom_call_target="tpu_custom_call" | custom-call | tf_op jit(solution)/shard_map/pallas_call | solution.py:495
  141.5 3.9 %cosine_convert_fusion = (bf16[512,512]{1,0:T(8,128)(2,1)S(1)}, bf16[512,512]{1,0:T(8,128)(2,1)S(1)}) fusion(f32[512,512]{1,0:T(8,128)S(1)} %shard_map.116, f32[]{:T(128)S(6)} %add.507), kind=kLoop, calls=%fused_computation.55 | loop fusion | flops 786432 | bytes 2097156 | tf_op jit(solution)/shard_map/convert.15
  146.0 0.5 convolution_bitcast_fusion.5
  146.9 1.4 convolution_bitcast_fusion.4
  148.7 0.5 convolution_bitcast_fusion.3
  149.2 1.2 copy.227
  150.7 0.5 fusion.1
  151.2 0.6 copy.150
  151.8 22.0 %shard_map.117 = bf16[2,32,8192]{2,1,0:T(8,128)(2,1)S(1)} custom-call(bf16[2,512,512]{2,1,0:T(8,128)(2,1)S(1)} %bitcast.176), custom_call_target="tpu_custom_call" | custom-call | tf_op jit(solution)/shard_map/pallas_call | solution.py:576
  174.0 0.5 convolution_bitcast_fusion.2
  174.8 0.4 convolution_bitcast_fusion.1
  175.6 0.5 convolution_bitcast_fusion
  176.4 0.5 fusion
  177.0 0.3 add.541
  177.4 1.1 fusion.135
  178.9 2.3 %gather_fusion = f32[512]{0:T(512)S(1)} fusion(f32[1024]{0:T(1024)S(1)} %multiply_bitcast_fusion, s32[1024]{0:T(1024)S(1)} %pad_clamp_fusion), kind=kCustom, calls=%fused_computation | custom fusion | bytes 6144 | tf_op jit(solution)/shard_map/jit(_take)/gather | solution.py:698
  181.6 0.6 copy.161
  182.2 16.0 %shard_map.118 = f32[1,128]{1,0:T(1,128)} custom-call(f32[8,4,1,128]{3,2,1,0:T(1,128)} %bitcast.186), custom_call_target="tpu_custom_call" | custom-call | tf_op jit(solution)/shard_map/pallas_call | solution.py:643
  198.2 1.3 multiply_bitcast_fusion.1
  (74 shorter events, 6.7 us)
Async XLA Ops:
  1.0 1.6 copy-start.1
  2.6 1.0 copy-start.2
  3.7 0.9 copy-start.3
  4.6 21.9 %copy-start.9 = (s32[1,2]{1,0:T(1,128)S(1)}, s32[1,2]{1,0:T(1,128)}, u32[]{:S(2)}) copy-start(s32[1,2]{1,0:T(1,128)} %param.11) | copy-start | bytes 28
  4.6 27.5 %copy-start.5 = (s32[1,512]{1,0:T(1,128)S(1)}, s32[1,512]{1,0:T(1,128)}, u32[]{:S(2)}) copy-start(s32[1,512]{1,0:T(1,128)} %param.13) | copy-start | bytes 6148
  26.0 14.3 %collective-permute-start.1 = (bf16[2,4,2,256,512]{4,3,2,1,0:T(8,128)(2,1)}, bf16[2,4,2,256,512]{4,3,2,1,0:T(8,128)(2,1)}, u32[]{:S(2)}, u32[]{:S(2)}) collective-permute-start(bf16[2,4,2,256,512]{4,3,2,1,0:T(8,128)(2,1)} %get-tuple-element.9), channel_id=1, source_target_pairs={{0,1},{1,0},{2,3},{3,2},{4,5},{5,4},{6,7},{7,6},{8,9},{9,8},{10,11... | collective-permute-start | bytes 12582920 | tf_op jit(solution)/shard_map/ppermute | solution.py:523
  27.0 6.8 %collective-permute-start = (s32[]{:T(128)}, s32[]{:T(128)}, u32[]{:S(2)}, u32[]{:S(2)}) collective-permute-start(s32[]{:T(128)} %bitcast.24), channel_id=1, source_target_pairs={{0,16},{16,0},{1,17},{17,1},{2,18},{18,2},{3,19},{19,3},{4,20},{20... | collective-permute-start | bytes 20 | tf_op jit(solution)/shard_map/ppermute | solution.py:525
  40.2 1.6 copy-start
  41.8 2.2 %copy-start.4 = (bf16[2,4,2,256,512]{4,3,2,1,0:T(8,128)(2,1)S(1)}, bf16[2,4,2,256,512]{4,3,2,1,0:T(8,128)(2,1)}, u32[]{:S(2)}) copy-start(bf16[2,4,2,256,512]{4,3,2,1,0:T(8,128)(2,1)} %get-tuple-element.8.kept) | copy-start | bytes 12582916
  177.3 3.9 %copy-start.7 = (f32[1,512]{1,0:T(1,128)S(1)}, f32[1,512]{1,0:T(1,128)}, u32[]{:S(2)}) copy-start(f32[1,512]{1,0:T(1,128)} %param.14) | copy-start | bytes 6148
  177.3 3.9 %copy-start.8 = (s32[512]{0:T(512)S(1)}, s32[512]{0:T(512)}, u32[]{:S(2)}) copy-start(s32[512]{0:T(512)} %param.15) | copy-start | bytes 6148
  178.9 20.6 %copy-start.6 = (f32[8,128]{1,0:T(8,128)}, f32[8,128]{1,0:T(8,128)S(1)}, u32[]{:S(2)}) copy-start(f32[8,128]{1,0:T(8,128)S(1)} %fusion.2) | copy-start | bytes 12292
